TPU v7x, 32 devices: a whole 2x2x4 slice. The times are simulated.
32 devices in a mesh: ctx: 16 (over z, y, core), fsdp: 2 (over x).
Axes of the slice: x: 2, y: 2, z: 4, core: 2. Of those that a mesh axis runs over, the one named last changes fastest.
Arguments:
- tokens: bfloat16 [4, 2048, 960], P('fsdp', 'ctx'), may hold values from -6 to 6
- cotangent: bfloat16 [4, 2048, 960], P('fsdp', 'ctx'), may hold values from -6 to 6
- early_block: int32 [4, 16], P('fsdp'), may hold values from 0 to 15, as said below
- positions: int32 [4, 2048], P('fsdp', 'ctx'), may hold values from 0 to 2047, as said below
- norm_gain: bfloat16 [960], P('fsdp'), may hold values from 0.5 to 1.5
- w_query: bfloat16 [960, 960], P('fsdp'), may hold values from -0.1875 to 0.1875
- w_key: bfloat16 [960, 320], P('fsdp'), may hold values from -0.1875 to 0.1875
- w_value: bfloat16 [960, 320], P('fsdp'), may hold values from -0.1875 to 0.1875
- w_out: bfloat16 [960, 960], P('fsdp'), may hold values from -1.5 to 1.5
- post_gain: bfloat16 [960], P('fsdp'), may hold values from 0.5 to 1.5
- w_gate: bfloat16 [960, 2560], P('fsdp'), may hold values from -0.1875 to 0.1875
- w_up: bfloat16 [960, 2560], P('fsdp'), may hold values from -0.1875 to 0.1875
- w_down: bfloat16 [2560, 960], P('fsdp'), may hold values from -0.125 to 0.125
Outputs:
- output: bfloat16 [4, 2048, 960], P('fsdp', 'ctx')
- grad_tokens: bfloat16 [4, 2048, 960], P('fsdp', 'ctx')
- grad_norm_gain: float32 [960], P('fsdp')
- grad_w_query: float32 [960, 960], P('fsdp')
- grad_w_key: float32 [960, 320], P('fsdp')
- grad_w_value: float32 [960, 320], P('fsdp')
- grad_w_out: float32 [960, 960], P('fsdp')
- grad_post_gain: float32 [960], P('fsdp')
- grad_w_gate: float32 [960, 2560], P('fsdp')
- grad_w_up: float32 [960, 2560], P('fsdp')
- grad_w_down: float32 [2560, 960], P('fsdp')
Inputs may be any that keep to these rules, and one draw needn't show every extreme that they name: Each row is an ordering of 0 to 15; index c of ctx holds blocks early_block[s, c] and 31 - early_block[s, c] of sequence s. `positions`: in sequence order each sequence is a pack of documents; a token's position is its distance from its document's first token, and each sequence begins a document; the first sequence is a single document.
All inputs are finite; a program needn't handle non-finite values.
Results may differ from a plain program's by a relative error of at most 0.015.
Values may be sent and summed in bfloat16 or wider, within the bound.
A program may use at most 256 MiB of HBM per device.

v0:
```python
import math

import jax
import jax.numpy as jnp
from jax import lax
from jax.sharding import PartitionSpec as P

H = 15
KVH = 5
HD = 64


EPSILON = 1e-05
MASKED = -1e30


def rope_tables(places, head_size):
    half_size = head_size // 2
    frequency = jnp.exp(
        jnp.arange(half_size, dtype=jnp.float32) * (-2.0 * math.log(10000.0) / head_size)
    )
    angles = places.astype(jnp.float32)[..., None] * frequency
    return (jnp.cos(angles), jnp.sin(angles))


def rotate(values, cosines, sines):
    half_size = values.shape[-1] // 2
    first_half = values[..., :half_size]
    second_half = values[..., half_size:]
    return jnp.concatenate(
        [first_half * cosines - second_half * sines, second_half * cosines + first_half * sines],
        axis=-1,
    )


def norm_scale(values):
    return lax.rsqrt(jnp.mean(values * values, axis=-1, keepdims=True) + EPSILON)


def norm_back(grad_normed, unit_rows, scale_rows, gain_row):
    weighted = grad_normed * gain_row
    return scale_rows * (
        weighted - unit_rows * jnp.mean(weighted * unit_rows, axis=-1, keepdims=True)
    )


def block_places(blocks, block_len):
    places = blocks[..., None] * block_len + jnp.arange(block_len, dtype=jnp.int32)
    return places.reshape(blocks.shape[:-1] + (2 * block_len,))


def block_scores(query_rows, key_block, query_places, key_places, factor):
    scores = (
        jnp.einsum("qhgd,khd->hgqk", query_rows, key_block, preferred_element_type=jnp.float32)
        * factor
    )
    allowed = key_places[None, :] <= query_places[:, None]
    return jnp.where(allowed, scores, MASKED)


def split_keys(key_all, value_all, key_places):
    total_rows, heads_kv, head_size = key_all.shape
    stride = math.gcd(total_rows, 1024)
    number = total_rows // stride
    return (
        key_all.reshape(number, stride, heads_kv, head_size),
        value_all.reshape(number, stride, heads_kv, head_size),
        key_places.reshape(number, stride),
    )


def attend_forward(query_rows, key_all, value_all, query_places, key_places, factor):
    key_blocks, value_blocks, place_blocks = split_keys(key_all, value_all, key_places)
    stat_shape = (query_rows.shape[1], query_rows.shape[2], query_rows.shape[0])

    def gather_stats(state, entries):
        running_max, total_sum = state
        key_block, place_block = entries
        scores = block_scores(query_rows, key_block, query_places, place_block, factor)
        new_max = jnp.maximum(running_max, jnp.max(scores, axis=-1))
        total_sum = total_sum * jnp.exp(running_max - new_max) + jnp.sum(
            jnp.exp(scores - new_max[..., None]), axis=-1
        )
        return ((new_max, total_sum), None)

    starting = (jnp.full(stat_shape, MASKED, jnp.float32), jnp.zeros(stat_shape, jnp.float32))
    (running_max, total_sum), _ = lax.scan(gather_stats, starting, (key_blocks, place_blocks))
    log_total = running_max + jnp.log(total_sum)

    def weigh(totals, entries):
        key_block, value_block, place_block = entries
        scores = block_scores(query_rows, key_block, query_places, place_block, factor)
        probability = jnp.exp(scores - log_total[..., None]).astype(jnp.bfloat16)
        return (
            totals
            + jnp.einsum(
                "hgqk,khd->qhgd", probability, value_block, preferred_element_type=jnp.float32
            ),
            None,
        )

    attended, _ = lax.scan(
        weigh, jnp.zeros(query_rows.shape, jnp.float32), (key_blocks, value_blocks, place_blocks)
    )
    return (attended, log_total)


def attend_backward(
    query_rows,
    grad_rows,
    log_total,
    delta_rows,
    key_all,
    value_all,
    query_places,
    key_places,
    factor,
):
    key_blocks, value_blocks, place_blocks = split_keys(key_all, value_all, key_places)

    def accumulate(totals, entries):
        key_block, value_block, place_block = entries
        scores = block_scores(query_rows, key_block, query_places, place_block, factor)
        probability = jnp.exp(scores - log_total[..., None])
        grad_probability = jnp.einsum(
            "qhgd,khd->hgqk", grad_rows, value_block, preferred_element_type=jnp.float32
        )
        grad_scores = (probability * (grad_probability - delta_rows[..., None])).astype(
            jnp.bfloat16
        )
        totals = (
            totals
            + jnp.einsum(
                "hgqk,khd->qhgd", grad_scores, key_block, preferred_element_type=jnp.float32
            )
            * factor
        )
        key_terms = (
            jnp.einsum(
                "hgqk,qhgd->khd", grad_scores, query_rows, preferred_element_type=jnp.float32
            )
            * factor
        )
        value_terms = jnp.einsum(
            "hgqk,qhgd->khd",
            probability.astype(jnp.bfloat16),
            grad_rows,
            preferred_element_type=jnp.float32,
        )
        return (totals, (key_terms, value_terms))

    grad_query, block_terms = lax.scan(
        accumulate,
        jnp.zeros(query_rows.shape, jnp.float32),
        (key_blocks, value_blocks, place_blocks),
    )
    return (grad_query, block_terms)


def on_device(
    tokens,
    cotangent,
    early_block,
    positions,
    norm_gain,
    w_query,
    w_key,
    w_value,
    w_out,
    post_gain,
    w_gate,
    w_up,
    w_down,
):
    (
        gain_one,
        query_weight,
        key_weight,
        value_weight,
        out_weight,
        gain_two,
        gate_weight,
        up_weight,
        down_weight,
    ) = (
        lax.all_gather(norm_gain, "fsdp", axis=0, tiled=True),
        lax.all_gather(w_query, "fsdp", axis=0, tiled=True),
        lax.all_gather(w_key, "fsdp", axis=0, tiled=True),
        lax.all_gather(w_value, "fsdp", axis=0, tiled=True),
        lax.all_gather(w_out, "fsdp", axis=0, tiled=True),
        lax.all_gather(post_gain, "fsdp", axis=0, tiled=True),
        lax.all_gather(w_gate, "fsdp", axis=0, tiled=True),
        lax.all_gather(w_up, "fsdp", axis=0, tiled=True),
        lax.all_gather(w_down, "fsdp", axis=0, tiled=True),
    )
    seq_count, rows_seq, model_width = tokens.shape
    block_len = rows_seq // 2
    devices = lax.axis_size("ctx")
    groups = H // KVH
    factor = HD ** (-0.5)
    flat_rows = tokens.reshape(-1, model_width).astype(jnp.float32)
    scale_one = norm_scale(flat_rows)
    unit_one = flat_rows * scale_one
    normed = (unit_one * gain_one.astype(jnp.float32)).astype(jnp.bfloat16)
    query_raw = jnp.dot(normed, query_weight, preferred_element_type=jnp.float32)
    key_raw = jnp.dot(normed, key_weight, preferred_element_type=jnp.float32)
    value_rows = jnp.dot(normed, value_weight, preferred_element_type=jnp.float32).astype(
        jnp.bfloat16
    )
    cosines, sines = rope_tables(positions.reshape(-1), HD)
    cosines = cosines[:, None, :]
    sines = sines[:, None, :]
    query_rot = (
        rotate(query_raw.reshape(-1, H, HD), cosines, sines)
        .astype(jnp.bfloat16)
        .reshape(seq_count, rows_seq, KVH, groups, HD)
    )
    key_rot = (
        rotate(key_raw.reshape(-1, KVH, HD), cosines, sines)
        .astype(jnp.bfloat16)
        .reshape(seq_count, rows_seq, KVH * HD)
    )
    value_seq = value_rows.reshape(seq_count, rows_seq, KVH * HD)
    ctx_place = lax.axis_index("ctx")
    own_early = jnp.sum(
        jnp.where(jnp.arange(devices, dtype=jnp.int32)[None, :] == ctx_place, early_block, 0),
        axis=1,
    )
    own_places = block_places(
        jnp.stack([own_early, 2 * devices - 1 - own_early], axis=-1), block_len
    )
    all_places = block_places(
        jnp.stack([early_block, 2 * devices - 1 - early_block], axis=-1), block_len
    ).reshape(seq_count, devices * rows_seq)
    key_gathered, value_gathered = (
        lax.all_gather(key_rot, "ctx", axis=1, tiled=True),
        lax.all_gather(value_seq, "ctx", axis=1, tiled=True),
    )
    attended_list = []
    total_list = []
    for sequence in range(seq_count):
        attended, log_total = attend_forward(
            query_rot[sequence],
            key_gathered[sequence].reshape(-1, KVH, HD),
            value_gathered[sequence].reshape(-1, KVH, HD),
            own_places[sequence],
            all_places[sequence],
            factor,
        )
        attended_list.append(attended)
        total_list.append(log_total)
    attended_all = jnp.stack(attended_list)
    mixed_rows = attended_all.reshape(-1, H * HD).astype(jnp.bfloat16)
    residual = flat_rows + jnp.dot(mixed_rows, out_weight, preferred_element_type=jnp.float32)
    scale_two = norm_scale(residual)
    unit_two = residual * scale_two
    normed_two = (unit_two * gain_two.astype(jnp.float32)).astype(jnp.bfloat16)
    gate_act = jnp.dot(normed_two, gate_weight, preferred_element_type=jnp.float32)
    up_act = jnp.dot(normed_two, up_weight, preferred_element_type=jnp.float32)
    sigmoid_gate = jax.nn.sigmoid(gate_act)
    hidden = (gate_act * sigmoid_gate * up_act).astype(jnp.bfloat16)
    output = (
        (residual + jnp.dot(hidden, down_weight, preferred_element_type=jnp.float32))
        .astype(jnp.bfloat16)
        .reshape(tokens.shape)
    )
    (
        gain_one_b,
        query_back,
        key_back,
        value_back,
        out_back,
        gain_two_b,
        gate_back,
        up_back,
        down_back,
    ) = (
        gain_one,
        query_weight,
        key_weight,
        value_weight,
        out_weight,
        gain_two,
        gate_weight,
        up_weight,
        down_weight,
    )
    grad_out = cotangent.reshape(-1, model_width)
    grad_hidden = jnp.dot(grad_out, down_back.T, preferred_element_type=jnp.float32)
    grad_down = jnp.dot(hidden.T, grad_out, preferred_element_type=jnp.float32)
    grad_up = (grad_hidden * gate_act * sigmoid_gate).astype(jnp.bfloat16)
    grad_gate = (
        grad_hidden * up_act * sigmoid_gate * (1.0 + gate_act * (1.0 - sigmoid_gate))
    ).astype(jnp.bfloat16)
    grad_gate_w = jnp.dot(normed_two.T, grad_gate, preferred_element_type=jnp.float32)
    grad_up_w = jnp.dot(normed_two.T, grad_up, preferred_element_type=jnp.float32)
    grad_normed_two = jnp.dot(grad_gate, gate_back.T, preferred_element_type=jnp.float32) + jnp.dot(
        grad_up, up_back.T, preferred_element_type=jnp.float32
    )
    grad_gain_two = jnp.sum(grad_normed_two * unit_two, axis=0)
    grad_residual = grad_out.astype(jnp.float32) + norm_back(
        grad_normed_two, unit_two, scale_two, gain_two_b.astype(jnp.float32)
    )
    grad_residual_low = grad_residual.astype(jnp.bfloat16)
    grad_out_w = jnp.dot(mixed_rows.T, grad_residual_low, preferred_element_type=jnp.float32)
    grad_mixed = (
        jnp.dot(grad_residual_low, out_back.T, preferred_element_type=jnp.float32)
        .astype(jnp.bfloat16)
        .reshape(seq_count, rows_seq, KVH, groups, HD)
    )
    grad_query_list = []
    grad_key_list = []
    grad_value_list = []
    for sequence in range(seq_count):
        grad_rows = grad_mixed[sequence]
        attended = attended_list[sequence]
        log_total = total_list[sequence]
        delta_rows = jnp.einsum("qhgd,qhgd->hgq", grad_rows.astype(jnp.float32), attended)
        key_all = key_gathered[sequence].reshape(-1, KVH, HD)
        value_all = value_gathered[sequence].reshape(-1, KVH, HD)
        grad_query, block_terms = attend_backward(
            query_rot[sequence],
            grad_rows,
            log_total,
            delta_rows,
            key_all,
            value_all,
            own_places[sequence],
            all_places[sequence],
            factor,
        )
        key_terms = block_terms[0].reshape(-1, KVH * HD)
        value_terms = block_terms[1].reshape(-1, KVH * HD)
        grad_key, grad_value = (
            lax.psum_scatter(key_terms, "ctx", scatter_dimension=0, tiled=True),
            lax.psum_scatter(value_terms, "ctx", scatter_dimension=0, tiled=True),
        )
        grad_key = grad_key.reshape(rows_seq, KVH, HD)
        grad_value = grad_value.reshape(rows_seq, KVH, HD)
        grad_query_list.append(grad_query)
        grad_key_list.append(grad_key)
        grad_value_list.append(grad_value)
    grad_query_raw = (
        rotate(jnp.stack(grad_query_list).reshape(-1, H, HD), cosines, -sines)
        .astype(jnp.bfloat16)
        .reshape(-1, H * HD)
    )
    grad_key_raw = (
        rotate(jnp.stack(grad_key_list).reshape(-1, KVH, HD), cosines, -sines)
        .astype(jnp.bfloat16)
        .reshape(-1, KVH * HD)
    )
    grad_value_low = jnp.stack(grad_value_list).reshape(-1, KVH * HD).astype(jnp.bfloat16)
    grad_query_w = jnp.dot(normed.T, grad_query_raw, preferred_element_type=jnp.float32)
    grad_key_w = jnp.dot(normed.T, grad_key_raw, preferred_element_type=jnp.float32)
    grad_value_w = jnp.dot(normed.T, grad_value_low, preferred_element_type=jnp.float32)
    grad_normed = (
        jnp.dot(grad_query_raw, query_back.T, preferred_element_type=jnp.float32)
        + jnp.dot(grad_key_raw, key_back.T, preferred_element_type=jnp.float32)
        + jnp.dot(grad_value_low, value_back.T, preferred_element_type=jnp.float32)
    )
    grad_gain_one = jnp.sum(grad_normed * unit_one, axis=0)
    grad_input = (
        (
            grad_residual
            + norm_back(grad_normed, unit_one, scale_one, gain_one_b.astype(jnp.float32))
        )
        .astype(jnp.bfloat16)
        .reshape(tokens.shape)
    )
    (
        owned_gain_one,
        owned_query,
        owned_key,
        owned_value,
        owned_out,
        owned_gain_two,
        owned_gate,
        owned_up,
        owned_down,
    ) = (
        lax.psum_scatter(
            grad_gain_one.astype(jnp.bfloat16), "fsdp", scatter_dimension=0, tiled=True
        ).astype(jnp.float32),
        lax.psum_scatter(
            grad_query_w.astype(jnp.bfloat16), "fsdp", scatter_dimension=0, tiled=True
        ).astype(jnp.float32),
        lax.psum_scatter(
            grad_key_w.astype(jnp.bfloat16), "fsdp", scatter_dimension=0, tiled=True
        ).astype(jnp.float32),
        lax.psum_scatter(
            grad_value_w.astype(jnp.bfloat16), "fsdp", scatter_dimension=0, tiled=True
        ).astype(jnp.float32),
        lax.psum_scatter(
            grad_out_w.astype(jnp.bfloat16), "fsdp", scatter_dimension=0, tiled=True
        ).astype(jnp.float32),
        lax.psum_scatter(
            grad_gain_two.astype(jnp.bfloat16), "fsdp", scatter_dimension=0, tiled=True
        ).astype(jnp.float32),
        lax.psum_scatter(
            grad_gate_w.astype(jnp.bfloat16), "fsdp", scatter_dimension=0, tiled=True
        ).astype(jnp.float32),
        lax.psum_scatter(
            grad_up_w.astype(jnp.bfloat16), "fsdp", scatter_dimension=0, tiled=True
        ).astype(jnp.float32),
        lax.psum_scatter(
            grad_down.astype(jnp.bfloat16), "fsdp", scatter_dimension=0, tiled=True
        ).astype(jnp.float32),
    )
    summed = lax.psum(
        (
            owned_gain_one,
            owned_query,
            owned_key,
            owned_value,
            owned_out,
            owned_gain_two,
            owned_gate,
            owned_up,
            owned_down,
        ),
        "ctx",
    )
    return (
        output,
        grad_input,
        summed[0],
        summed[1],
        summed[2],
        summed[3],
        summed[4],
        summed[5],
        summed[6],
        summed[7],
        summed[8],
    )


def solution(mesh):
    placed = (
        P("fsdp", "ctx", None),
        P("fsdp", "ctx", None),
        P("fsdp", None),
        P("fsdp", "ctx"),
        P("fsdp"),
        P("fsdp", None),
        P("fsdp", None),
        P("fsdp", None),
        P("fsdp", None),
        P("fsdp"),
        P("fsdp", None),
        P("fsdp", None),
        P("fsdp", None),
    )
    return jax.shard_map(
        on_device,
        mesh=mesh,
        in_specs=placed,
        out_specs=(
            P("fsdp", "ctx", None),
            P("fsdp", "ctx", None),
            P("fsdp"),
            P("fsdp", None),
            P("fsdp", None),
            P("fsdp", None),
            P("fsdp", None),
            P("fsdp"),
            P("fsdp", None),
            P("fsdp", None),
            P("fsdp", None),
        ),
        check_vma=False,
    )
```

profile of v0, /device:TPU:1, one launch (start us, length us, event | category | flops | bytes accessed | tf_op | source)
XLA Modules:
  0.0 1588.1 jit_solution(4924305198764464597)
XLA Ops:
  12.9 4.3 all-reduce.6
  20.0 16.5 %all-gather.1 = bf16[2,480,320]{1,2,0:T(8,128)(2,1)S(1)} all-gather(bf16[1,480,320]{1,2,0:T(8,128)(2,1)S(1)} %bitcast.590), channel_id=1, replica_groups=mesh['ctx'=16,'fsdp'=2] {'fsdp'}, dimensions={0}, use_global_device_ids=true | all-gather | bytes 921600 | tf_op jit(solution)/shard_map/all_gather | solution.py:188
  39.9 16.6 %all-gather = bf16[2,480,320]{1,2,0:T(8,128)(2,1)S(1)} all-gather(bf16[1,480,320]{1,2,0:T(8,128)(2,1)S(1)} %bitcast.591), channel_id=1, replica_groups=mesh['ctx'=16,'fsdp'=2] {'fsdp'}, dimensions={0}, use_global_device_ids=true | all-gather | bytes 921600 | tf_op jit(solution)/shard_map/all_gather | solution.py:189
  63.2 2.8 copy.97
  67.7 35.5 %all-gather.12.cloned.1.call-done = bf16[2,2048,320]{1,2,0:T(8,128)(2,1)} async-done(((bf16[2,128,320]{1,2,0:T(8,128)(2,1)}), bf16[2,2048,320]{1,2,0:T(8,128)(2,1)}) %all-gather.12.cloned.1.call-update) | async-done | bytes 2621456 | tf_op jit(solution)/shard_map/all_gather | solution.py:236
  108.7 39.9 %all-gather.10.cloned.1.call-done = bf16[2,2048,320]{1,2,0:T(8,128)(2,1)} async-done(((bf16[2,128,320]{1,2,0:T(8,128)(2,1)}), bf16[2,2048,320]{1,2,0:T(8,128)(2,1)}) %all-gather.10.cloned.1.call-update) | async-done | bytes 2621456 | tf_op jit(solution)/shard_map/all_gather | solution.py:237
  148.6 3.5 fusion.150
  152.1 4.4 reshape_reshape_squeeze.16
  156.5 2.8 copy.99
  159.3 4.4 reshape_reshape_squeeze.18
  163.7 2.7 copy.102
  169.9 8.3 while.80
  178.2 6.6 while.78
  184.8 9.7 while.81
  185.1 4.4 fusion.279
  189.7 4.8 fusion.279
  194.5 9.5 while.79
  194.7 4.4 fusion.271
  199.3 4.5 fusion.271
  207.1 2.7 multiply_reduce_fusion.4
  211.1 35.0 %all-gather.20.cloned.1.call-done = bf16[960,2560]{1,0:T(8,128)(2,1)} async-done(((bf16[480,2560]{1,0:T(8,128)(2,1)}), bf16[960,2560]{1,0:T(8,128)(2,1)}) %all-gather.20.cloned.1.call-update) | async-done | bytes 4915216 | tf_op jit(solution)/shard_map/all_gather | solution.py:193
  246.1 5.4 fusion.158
  251.5 60.9 %all-gather.18.cloned.1.call-done = bf16[960,2560]{1,0:T(8,128)(2,1)} async-done(((bf16[480,2560]{1,0:T(8,128)(2,1)}), bf16[960,2560]{1,0:T(8,128)(2,1)}) %all-gather.18.cloned.1.call-update) | async-done | bytes 4915216 | tf_op jit(solution)/shard_map/all_gather | solution.py:192
  312.4 5.4 fusion.157
  317.8 61.0 %all-gather.22.cloned.1.call-done = bf16[2560,960]{0,1:T(8,128)(2,1)} async-done(((bf16[1280,960]{0,1:T(8,128)(2,1)}), bf16[2560,960]{0,1:T(8,128)(2,1)}) %all-gather.22.cloned.1.call-update) | async-done | bytes 4915216 | tf_op jit(solution)/shard_map/all_gather | solution.py:194
  378.9 7.0 multiply_convert_fusion
  387.8 4.6 multiply_reduce_fusion
  402.3 124.7 %while.83 = (s32[]{:T(128)}, f32[128,5,3,64]{0,3,2,1:T(8,128)}, f32[2,1024,5,64]{1,0,3,2:T(2,128)}, f32[2,1024,5,64]{1,0,3,2:T(2,128)}, bf16[2,1024,5,64]{1,3,2,...) while((s32[]{:T(128)}, f32[128,5,3,64]{0,3,2,1:T(8,128)}, ...), condition=%wide.region_19.20_spmd.clone, body=%wide.region_18.19_spmd.clone.sunk | while | flops 1278779392 | bytes 67276056 | solution.py:152
  405.3 3.0 fusion.309
  408.3 3.7 fusion.306
  418.2 23.3 %dynamic_update_slice.23 = f32[2,1024,5,64]{1,0,3,2:T(2,128)} dynamic-update-slice(f32[2,1024,5,64]{1,0,3,2:T(2,128)} %get-tuple-element.1283, f32[1,1024,5,64]{1,0,3,2:T(1,128)S(1)} %copy.254, s32[]{:T(128)S(6)} %copy.296, s32[]{:T(128)} %constant.111.clone.1..sunk.5, s32[]{:T(128)} %constant.111.clone.1..sunk.5, s32[]{:T(128)} %constant.111.clone.1..sunk.5) | dynamic-update-slice | bytes 2621444 | tf_op jit(solution)/shard_map/while/body/jit(dynamic_update_index_in_dim)/dynamic_update_slice | solution.py:152
  441.4 23.4 %dynamic_update_slice.24 = f32[2,1024,5,64]{1,0,3,2:T(2,128)} dynamic-update-slice(f32[2,1024,5,64]{1,0,3,2:T(2,128)} %get-tuple-element.1284, f32[1,1024,5,64]{1,0,3,2:T(1,128)S(1)} %copy.255, s32[]{:T(128)S(6)} %copy.296, s32[]{:T(128)} %constant.111.clone.1..sunk.5, s32[]{:T(128)} %constant.111.clone.1..sunk.5, s32[]{:T(128)} %constant.111.clone.1..sunk.5) | dynamic-update-slice | bytes 2621444 | tf_op jit(solution)/shard_map/while/body/jit(dynamic_update_index_in_dim)/dynamic_update_slice | solution.py:152
  467.5 3.0 fusion.309
  470.4 3.7 fusion.306
  480.3 23.3 %dynamic_update_slice.23 = f32[2,1024,5,64]{1,0,3,2:T(2,128)} dynamic-update-slice(f32[2,1024,5,64]{1,0,3,2:T(2,128)} %get-tuple-element.1283, f32[1,1024,5,64]{1,0,3,2:T(1,128)S(1)} %copy.254, s32[]{:T(128)S(6)} %copy.296, s32[]{:T(128)} %constant.111.clone.1..sunk.5, s32[]{:T(128)} %constant.111.clone.1..sunk.5, s32[]{:T(128)} %constant.111.clone.1..sunk.5) | dynamic-update-slice | bytes 2621444 | tf_op jit(solution)/shard_map/while/body/jit(dynamic_update_index_in_dim)/dynamic_update_slice | solution.py:152
  503.6 23.4 %dynamic_update_slice.24 = f32[2,1024,5,64]{1,0,3,2:T(2,128)} dynamic-update-slice(f32[2,1024,5,64]{1,0,3,2:T(2,128)} %get-tuple-element.1284, f32[1,1024,5,64]{1,0,3,2:T(1,128)S(1)} %copy.255, s32[]{:T(128)S(6)} %copy.296, s32[]{:T(128)} %constant.111.clone.1..sunk.5, s32[]{:T(128)} %constant.111.clone.1..sunk.5, s32[]{:T(128)} %constant.111.clone.1..sunk.5) | dynamic-update-slice | bytes 2621444 | tf_op jit(solution)/shard_map/while/body/jit(dynamic_update_index_in_dim)/dynamic_update_slice | solution.py:152
  527.0 4.4 copy.184
  536.4 119.7 %while.82 = (s32[]{:T(128)}, f32[128,5,3,64]{0,3,2,1:T(8,128)}, f32[2,1024,5,64]{1,0,3,2:T(2,128)}, f32[2,1024,5,64]{1,0,3,2:T(2,128)}, bf16[2,1024,5,64]{1,3,2,...) while((s32[]{:T(128)}, f32[128,5,3,64]{0,3,2,1:T(8,128)}, ...), condition=%wide.region_17.18_spmd.clone, body=%wide.region_16.17_spmd.clone.sunk | while | flops 1278779392 | bytes 62033160 | solution.py:152
  537.8 3.0 fusion.294
  540.8 3.8 fusion.291
  549.6 23.3 %dynamic_update_slice.21 = f32[2,1024,5,64]{1,0,3,2:T(2,128)} dynamic-update-slice(f32[2,1024,5,64]{1,0,3,2:T(2,128)} %get-tuple-element.1325, f32[1,1024,5,64]{1,0,3,2:T(1,128)S(1)} %copy.252, s32[]{:T(128)S(6)} %copy.308, s32[]{:T(128)} %constant.111.clone.1..sunk.4, s32[]{:T(128)} %constant.111.clone.1..sunk.4, s32[]{:T(128)} %constant.111.clone.1..sunk.4) | dynamic-update-slice | bytes 2621444 | tf_op jit(solution)/shard_map/while/body/jit(dynamic_update_index_in_dim)/dynamic_update_slice | solution.py:152
  572.9 23.4 %dynamic_update_slice.22 = f32[2,1024,5,64]{1,0,3,2:T(2,128)} dynamic-update-slice(f32[2,1024,5,64]{1,0,3,2:T(2,128)} %get-tuple-element.1326, f32[1,1024,5,64]{1,0,3,2:T(1,128)S(1)} %copy.253, s32[]{:T(128)S(6)} %copy.308, s32[]{:T(128)} %constant.111.clone.1..sunk.4, s32[]{:T(128)} %constant.111.clone.1..sunk.4, s32[]{:T(128)} %constant.111.clone.1..sunk.4) | dynamic-update-slice | bytes 2621444 | tf_op jit(solution)/shard_map/while/body/jit(dynamic_update_index_in_dim)/dynamic_update_slice | solution.py:152
  597.7 3.0 fusion.294
  600.7 3.7 fusion.291
  609.4 23.3 %dynamic_update_slice.21 = f32[2,1024,5,64]{1,0,3,2:T(2,128)} dynamic-update-slice(f32[2,1024,5,64]{1,0,3,2:T(2,128)} %get-tuple-element.1325, f32[1,1024,5,64]{1,0,3,2:T(1,128)S(1)} %copy.252, s32[]{:T(128)S(6)} %copy.308, s32[]{:T(128)} %constant.111.clone.1..sunk.4, s32[]{:T(128)} %constant.111.clone.1..sunk.4, s32[]{:T(128)} %constant.111.clone.1..sunk.4) | dynamic-update-slice | bytes 2621444 | tf_op jit(solution)/shard_map/while/body/jit(dynamic_update_index_in_dim)/dynamic_update_slice | solution.py:152
  632.7 23.4 %dynamic_update_slice.22 = f32[2,1024,5,64]{1,0,3,2:T(2,128)} dynamic-update-slice(f32[2,1024,5,64]{1,0,3,2:T(2,128)} %get-tuple-element.1326, f32[1,1024,5,64]{1,0,3,2:T(1,128)S(1)} %copy.253, s32[]{:T(128)S(6)} %copy.308, s32[]{:T(128)} %constant.111.clone.1..sunk.4, s32[]{:T(128)} %constant.111.clone.1..sunk.4, s32[]{:T(128)} %constant.111.clone.1..sunk.4) | dynamic-update-slice | bytes 2621444 | tf_op jit(solution)/shard_map/while/body/jit(dynamic_update_index_in_dim)/dynamic_update_slice | solution.py:152
  656.1 4.4 copy.183
  662.3 2.6 copy.182
  679.0 44.1 %reduce-scatter.20.cloned.1.call-done = f32[128,320]{0,1:T(8,128)} async-done(((f32[2048,320]{0,1:T(8,128)}), f32[128,320]{0,1:T(8,128)}) %reduce-scatter.20.cloned.1.call-update) | async-done | bytes 163856 | tf_op jit(solution)/shard_map/reduce_scatter | solution.py:336
  726.1 64.2 %reduce-scatter.18.cloned.1.call-done = f32[128,320]{0,1:T(8,128)} async-done(((f32[2048,320]{0,1:T(8,128)}), f32[128,320]{0,1:T(8,128)}) %reduce-scatter.18.cloned.1.call-update) | async-done | bytes 163856 | tf_op jit(solution)/shard_map/reduce_scatter | solution.py:335
  790.3 67.3 %reduce-scatter.16.cloned.1.call-done = f32[128,320]{0,1:T(8,128)} async-done(((f32[2048,320]{0,1:T(8,128)}), f32[128,320]{0,1:T(8,128)}) %reduce-scatter.16.cloned.1.call-update) | async-done | bytes 163856 | tf_op jit(solution)/shard_map/reduce_scatter | solution.py:335
  860.9 5.0 convolution_convert_fusion
  866.9 5.2 convolution_convert_fusion.1
  872.5 5.0 convolution_convert_fusion.2
  878.7 4.5 fusion.115
  885.7 5.4 reduce-scatter.26.cloned.1.call-done
  891.1 33.3 %reduce-scatter.24.cloned.1.call-done = bf16[480,960]{1,0:T(8,128)(2,1)} async-done(((bf16[960,960]{1,0:T(8,128)(2,1)}), bf16[480,960]{1,0:T(8,128)(2,1)}) %reduce-scatter.24.cloned.1.call-update) | async-done | bytes 921616 | tf_op jit(solution)/shard_map/reduce_scatter | solution.py:385
  927.9 3.8 all-reduce.5
  932.9 10.5 reduce-scatter.36.cloned.1.call-done
  944.5 18.0 %reduce-scatter.34.cloned.1.call-done = bf16[480,320]{1,0:T(8,128)(2,1)} async-done(((bf16[960,320]{1,0:T(8,128)(2,1)}), bf16[480,320]{1,0:T(8,128)(2,1)}) %reduce-scatter.34.cloned.1.call-update) | async-done | bytes 307216
  963.7 63.8 %reduce-scatter.32.cloned.1.call-done = bf16[1280,960]{0,1:T(8,128)(2,1)} async-done(((bf16[2560,960]{0,1:T(8,128)(2,1)}), bf16[1280,960]{0,1:T(8,128)(2,1)}) %reduce-scatter.32.cloned.1.call-update) | async-done | bytes 2457616 | tf_op jit(solution)/shard_map/reduce_scatter | solution.py:406
  1027.4 64.9 %reduce-scatter.30.cloned.1.call-done = bf16[480,2560]{1,0:T(8,128)(2,1)} async-done(((bf16[960,2560]{1,0:T(8,128)(2,1)}), bf16[480,2560]{1,0:T(8,128)(2,1)}) %reduce-scatter.30.cloned.1.call-update) | async-done | bytes 2457616 | tf_op jit(solution)/shard_map/reduce_scatter | solution.py:403
  1092.3 64.9 %reduce-scatter.28.cloned.1.call-done = bf16[480,2560]{1,0:T(8,128)(2,1)} async-done(((bf16[960,2560]{1,0:T(8,128)(2,1)}), bf16[480,2560]{1,0:T(8,128)(2,1)}) %reduce-scatter.28.cloned.1.call-update) | async-done | bytes 2457616 | tf_op jit(solution)/shard_map/reduce_scatter | solution.py:400
  1157.3 423.6 %all-reduce.8 = (f32[480]{0:T(512)}, f32[480,960]{1,0:T(8,128)}, f32[480,320]{0,1:T(8,128)}, f32[480,320]{0,1:T(8,128)}, f32[480,960]{1,0:T(8,128)}, /*index=5*/...) all-reduce(f32[480]{0:T(512)S(1)} %dynamic-slice_convert_fusion.1, ...), channel_id=1, replica_groups=mesh['ctx'=16,'fsdp'=2] {'ctx'}, use_global_device_ids=true, to_apply=%region_27.28 | all-reduce | flops 4916160 | bytes 29498880 | tf_op jit(solution)/shard_map/psum | solution.py:410
  (328 shorter events, 127.6 us)
Async XLA Ops:
  7.2 371.7 %copy-start = (bf16[2,128,960]{1,2,0:T(8,128)(2,1)S(1)}, bf16[2,128,960]{1,2,0:T(8,128)(2,1)}, u32[]{:S(2)}) copy-start(bf16[2,128,960]{1,2,0:T(8,128)(2,1)} %param.26) | copy-start | bytes 1474564
  7.2 12.8 copy-start.42
  7.2 55.9 %all-gather.14.cloned.1.call-start = ((), (), s32[]{:S(2)}) async-start(), calls=%async_computation.13 | async-start | bytes 2949120 | tf_op jit(solution)/shard_map/all_gather | solution.py:187
  7.9 95.2 %all-gather.12.cloned.1.call-start = ((), (), s32[]{:S(2)}) async-start(), calls=%async_computation.12 | async-start | bytes 2785280 | tf_op jit(solution)/shard_map/all_gather | solution.py:236
  17.3 40.6 %copy-start.45 = (f32[960]{0:T(1024)}, f32[960]{0:T(1024)S(1)}, u32[]{:S(2)}) copy-start(f32[960]{0:T(1024)S(1)} %convert_element_type.202) | copy-start | bytes 11524
  17.3 40.6 %copy-start.47 = (f32[256]{0:T(256)}, f32[256]{0:T(256)S(1)}, u32[]{:S(2)}) copy-start(f32[256]{0:T(256)S(1)} %get-tuple-element.804) | copy-start | bytes 3076
  19.1 18.7 %copy-start.53 = (s32[2,128]{1,0:T(2,128)S(1)}, s32[2,128]{1,0:T(2,128)}, u32[]{:S(2)}) copy-start(s32[2,128]{1,0:T(2,128)} %param.28) | copy-start | bytes 3076
  37.2 2.8 copy-start.43
  38.7 28.0 %copy-start.36 = (f32[256,32]{0,1:T(8,128)}, f32[256,32]{0,1:T(8,128)S(1)}, u32[]{:S(2)}) copy-start(f32[256,32]{0,1:T(8,128)S(1)} %get-tuple-element.802) | copy-start | bytes 98308
  39.0 18.9 %copy-start.17 = (bf16[2,128,960]{1,2,0:T(8,128)(2,1)S(1)}, bf16[2,128,960]{1,2,0:T(8,128)(2,1)}, u32[]{:S(2)}) copy-start(bf16[2,128,960]{1,2,0:T(8,128)(2,1)} %param.25) | copy-start | bytes 1474564
  39.9 108.7 %all-gather.10.cloned.1.call-start = ((), (), s32[]{:S(2)}) async-start(), calls=%async_computation.11 | async-start | bytes 2785280 | tf_op jit(solution)/shard_map/all_gather | solution.py:237
  57.9 2.4 copy-start.26
  59.1 148.0 %all-gather.16.cloned.1.call-start = ((), (), s32[]{:S(2)}) async-start(), calls=%async_computation.14 | async-start | bytes 2949120 | tf_op jit(solution)/shard_map/all_gather | solution.py:190
  59.7 186.5 %all-gather.20.cloned.1.call-start = ((), (), s32[]{:S(2)}) async-start(), calls=%async_computation.16 | async-start | bytes 7372800 | tf_op jit(solution)/shard_map/all_gather | solution.py:193
  60.3 2.0 copy-start.51
  60.3 252.1 %all-gather.18.cloned.1.call-start = ((), (), s32[]{:S(2)}) async-start(), calls=%async_computation.15 | async-start | bytes 7372800 | tf_op jit(solution)/shard_map/all_gather | solution.py:192
  60.8 318.0 %all-gather.22.cloned.1.call-start = ((), (), s32[]{:S(2)}) async-start(), calls=%async_computation.17 | async-start | bytes 7372800 | tf_op jit(solution)/shard_map/all_gather | solution.py:194
  61.6 617.4 %reduce-scatter.22.cloned.1.call-start = ((), (), s32[]{:S(2)}) async-start(), calls=%async_computation.21 | async-start | bytes 2785280 | tf_op jit(solution)/shard_map/reduce_scatter | solution.py:336
  204.0 5.8 copy-start.1
  211.1 101.4 %copy-start.12 = (bf16[256,960]{0,1:T(8,128)(2,1)}, bf16[256,960]{0,1:T(8,128)(2,1)S(1)}, u32[]{:S(2)}) copy-start(bf16[256,960]{0,1:T(8,128)(2,1)S(1)} %multiply_convert_fusion.3) | copy-start | bytes 1474564
  378.9 7.0 copy-start.16
  385.9 1.9 copy-start.24
  392.4 1.5 copy-start.28
  393.9 3.6 copy-start.14
  393.9 1.5 copy-start.29
  393.9 2.5 copy-start.31
  402.7 10.7 copy-start.4
  414.3 2.5 copy-start.10
  441.4 23.4 %copy-start.5 = (bf16[2,1024,5,64]{1,3,2,0:T(8,128)(2,1)S(1)}, bf16[2,1024,5,64]{1,3,2,0:T(8,128)(2,1)}, u32[]{:S(2)}) copy-start(bf16[2,1024,5,64]{1,3,2,0:T(8,128)(2,1)} %copy-done.4) | copy-start | bytes 3932164 | tf_op jit(solution)/shard_map/while
  464.8 10.7 copy-start.4
  476.4 2.5 copy-start.10
  503.6 23.4 %copy-start.5 = (bf16[2,1024,5,64]{1,3,2,0:T(8,128)(2,1)S(1)}, bf16[2,1024,5,64]{1,3,2,0:T(8,128)(2,1)}, u32[]{:S(2)}) copy-start(bf16[2,1024,5,64]{1,3,2,0:T(8,128)(2,1)} %copy-done.4) | copy-start | bytes 3932164 | tf_op jit(solution)/shard_map/while
  531.4 191.8 %reduce-scatter.20.cloned.1.call-start = ((), (), s32[]{:S(2)}) async-start(), calls=%async_computation.20 | async-start | bytes 2785280 | tf_op jit(solution)/shard_map/reduce_scatter | solution.py:336
  531.6 4.8 copy-start.2
  572.9 23.4 %copy-start.3 = (bf16[2,1024,5,64]{1,3,2,0:T(8,128)(2,1)S(1)}, bf16[2,1024,5,64]{1,3,2,0:T(8,128)(2,1)}, u32[]{:S(2)}) copy-start(bf16[2,1024,5,64]{1,3,2,0:T(8,128)(2,1)} %get-tuple-element.1385) | copy-start | bytes 3932164 | tf_op jit(solution)/shard_map/while
  632.7 23.4 %copy-start.3 = (bf16[2,1024,5,64]{1,3,2,0:T(8,128)(2,1)S(1)}, bf16[2,1024,5,64]{1,3,2,0:T(8,128)(2,1)}, u32[]{:S(2)}) copy-start(bf16[2,1024,5,64]{1,3,2,0:T(8,128)(2,1)} %get-tuple-element.1385) | copy-start | bytes 3932164 | tf_op jit(solution)/shard_map/while
  660.5 1.7 copy-start.20
  660.6 129.7 %reduce-scatter.18.cloned.1.call-start = ((), (), s32[]{:S(2)}) async-start(), calls=%async_computation.19 | async-start | bytes 2785280 | tf_op jit(solution)/shard_map/reduce_scatter | solution.py:335
  664.9 1.8 copy-start.19
  664.9 192.6 %reduce-scatter.16.cloned.1.call-start = ((), (), s32[]{:S(2)}) async-start(), calls=%async_computation.18 | async-start | bytes 2785280 | tf_op jit(solution)/shard_map/reduce_scatter | solution.py:335
  669.3 3.4 copy-start.8
  669.3 3.4 copy-start.11
  669.4 221.7 %reduce-scatter.26.cloned.1.call-start = ((), (), s32[]{:S(2)}) async-start(), calls=%async_computation.23 | async-start | bytes 2949120 | tf_op jit(solution)/shard_map/reduce_scatter | solution.py:394
  672.7 251.7 %reduce-scatter.24.cloned.1.call-start = ((), (), s32[]{:S(2)}) async-start(), calls=%async_computation.22 | async-start | bytes 2949120 | tf_op jit(solution)/shard_map/reduce_scatter | solution.py:385
  672.8 3.9 copy-start.37
  672.8 3.9 copy-start.44
  674.6 2.3 copy-start.18
  674.6 2.3 copy-start.46
  674.6 2.3 copy-start.50
  676.9 47.3 %copy-start.32 = (bf16[256,15,64]{0,2,1:T(8,128)(2,1)}, bf16[256,15,64]{0,2,1:T(8,128)(2,1)S(1)}, u32[]{:S(2)}) copy-start(bf16[256,15,64]{0,2,1:T(8,128)(2,1)S(1)} %maximum_convert_fusion) | copy-start | bytes 1474564
  678.9 264.5 %reduce-scatter.36.cloned.1.call-start = ((), (), s32[]{:S(2)}) async-start(), calls=%async_computation.28 | async-start | bytes 1105920
  724.4 133.1 %copy-start.38 = (bf16[2,128,5,64]{1,0,3,2:T(2,128)(2,1)}, bf16[2,128,5,64]{1,0,3,2:T(2,128)(2,1)S(1)}, u32[]{:S(2)}) copy-start(bf16[2,128,5,64]{1,0,3,2:T(2,128)(2,1)S(1)} %copy.117) | copy-start | bytes 491524
  726.0 236.5 %reduce-scatter.34.cloned.1.call-start = ((), (), s32[]{:S(2)}) async-start(), calls=%async_computation.27 | async-start | bytes 1105920
  859.2 1.7 copy-start.40
  860.8 166.6 %reduce-scatter.32.cloned.1.call-start = ((), (), s32[]{:S(2)}) async-start(), calls=%async_computation.26 | async-start | bytes 7372800 | tf_op jit(solution)/shard_map/reduce_scatter | solution.py:406
  865.9 226.4 %reduce-scatter.30.cloned.1.call-start = ((), (), s32[]{:S(2)}) async-start(), calls=%async_computation.25 | async-start | bytes 7372800 | tf_op jit(solution)/shard_map/reduce_scatter | solution.py:403
  872.2 285.1 %reduce-scatter.28.cloned.1.call-start = ((), (), s32[]{:S(2)}) async-start(), calls=%async_computation.24 | async-start | bytes 7372800 | tf_op jit(solution)/shard_map/reduce_scatter | solution.py:400
  878.7 5.3 copy-start.27
  878.7 5.3 copy-start.33
  884.0 40.4 %copy-start.22 = (bf16[960,320]{0,1:T(8,128)(2,1)S(1)}, bf16[960,320]{0,1:T(8,128)(2,1)}, u32[]{:S(2)}) copy-start(bf16[960,320]{0,1:T(8,128)(2,1)} %copy-done.21) | copy-start | bytes 1843204
  884.0 40.4 %copy-start.41 = (bf16[256,5,64]{0,2,1:T(8,128)(2,1)S(1)}, bf16[256,5,64]{0,2,1:T(8,128)(2,1)}, u32[]{:S(2)}) copy-start(bf16[256,5,64]{0,2,1:T(8,128)(2,1)} %copy-done.40) | copy-start | bytes 491524
  885.7 40.4 %copy-start.39 = (bf16[2,128,5,64]{1,0,3,2:T(2,128)(2,1)S(1)}, bf16[2,128,5,64]{1,0,3,2:T(2,128)(2,1)}, u32[]{:S(2)}) copy-start(bf16[2,128,5,64]{1,0,3,2:T(2,128)(2,1)} %copy-done.38) | copy-start | bytes 491524
  885.7 40.4 %copy-start.48 = (f32[256]{0:T(256)S(1)}, f32[256]{0:T(256)}, u32[]{:S(2)}) copy-start(f32[256]{0:T(256)} %copy-done.47) | copy-start | bytes 3076
  885.7 42.2 %copy-start.52 = (bf16[960]{0:T(1024)(128)(2,1)S(1)}, bf16[960]{0:T(1024)(128)(2,1)}, u32[]{:S(2)}) copy-start(bf16[960]{0:T(1024)(128)(2,1)} %get-tuple-element.648) | copy-start | bytes 5764
  (15 other events, 19.0 us)
Sparse Core Ops, SparseCore 0:
  9.6 46.4 all-gather.13
  58.8 44.3 all-gather.11
  105.9 42.6 all-gather.9
  150.0 29.7 all-gather.15
  181.2 64.8 all-gather.19
  247.5 64.8 all-gather.17
  314.0 64.8 all-gather.21
  531.5 62.4 reduce-scatter.21
  660.7 62.4 reduce-scatter.19
  727.3 62.8 reduce-scatter.17
  794.6 62.8 reduce-scatter.15
  860.2 30.8 reduce-scatter.25
  894.0 30.3 reduce-scatter.23
  926.5 16.8 reduce-scatter.35
  945.5 16.9 reduce-scatter.33
  965.3 62.1 reduce-scatter.31
  1030.2 62.1 reduce-scatter.29
  1095.1 62.1 reduce-scatter.27
where the time goes:
time: 1610 us; the launch traced here: 1590 us
  waiting for transfers between devices  672 us (42%)
  blocking collectives  465 us (29%)
  local copies, waits for them, and re-layouts  280 us (17%)
  matrix products  129 us (8%)
  other arithmetic  21.7 us (1%)
  between operations  17 us (1%)
    psum x1, blocking collectives, on_device(): lax.psum((owned_gain_one, owned_query, owned_key, owned_value, owned_out,...  424 us
    dynamic_update_slice x16, local copies, waits for them, and re-layouts, attend_backward(): lax.scan(accumulate, jnp.zeros(query_rows.shape, jnp.float32), (key_block...  197 us
    reduce_scatter x2, waiting for transfers between devices, on_device(): lax.psum_scatter(key_terms, 'ctx', scatter_dimension=0, tiled=True)  131 us
    reduce_scatter x1, waiting for transfers between devices, on_device(): lax.psum_scatter(grad_gate_w.astype(jnp.bfloat16), 'fsdp', scatter_dimens...  64.9 us
    reduce_scatter x1, waiting for transfers between devices, on_device(): lax.psum_scatter(grad_up_w.astype(jnp.bfloat16), 'fsdp', scatter_dimensio...  64.9 us
    reduce_scatter x1, waiting for transfers between devices, on_device(): lax.psum_scatter(grad_down.astype(jnp.bfloat16), 'fsdp', scatter_dimensio...  63.8 us
    all_gather x1, waiting for transfers between devices, on_device(): lax.all_gather(w_down, 'fsdp', axis=0, tiled=True)  61 us
    all_gather x1, waiting for transfers between devices, on_device(): lax.all_gather(w_gate, 'fsdp', axis=0, tiled=True)  60.9 us
  transfers between devices with their start and end apart: 18, of which 15 were waited for; matrix products, arithmetic and copies ran while one was open for 17% of the time, Pallas kernels for 0%

commit v1 on v0

v1 whole, which is shorter than its diff:
```python
import math

import jax
import jax.numpy as jnp
from jax import lax
from jax.experimental import pallas as pl
from jax.experimental.pallas import tpu as pltpu
from jax.sharding import PartitionSpec as P

H = 15
KVH = 5
HD = 64


EPSILON = 1e-05
MASKED = -1e30


def rope_tables(places, head_size):
    half_size = head_size // 2
    frequency = jnp.exp(
        jnp.arange(half_size, dtype=jnp.float32) * (-2.0 * math.log(10000.0) / head_size)
    )
    angles = places.astype(jnp.float32)[..., None] * frequency
    return (jnp.cos(angles), jnp.sin(angles))


def rotate(values, cosines, sines):
    half = HD // 2
    width = values.shape[-1]
    ahead = jnp.concatenate([values[:, half:], values[:, :half]], axis=1)
    behind = jnp.concatenate([values[:, width - half :], values[:, : width - half]], axis=1)
    low = (jnp.arange(width, dtype=jnp.int32) % HD < half)[None, :]
    return values * cosines[:, :width] + jnp.where(low, -ahead, behind) * sines[:, :width]


def norm_scale(values):
    return lax.rsqrt(jnp.mean(values * values, axis=-1, keepdims=True) + EPSILON)


def norm_back(grad_normed, unit_rows, scale_rows, gain_row):
    weighted = grad_normed * gain_row
    return scale_rows * (
        weighted - unit_rows * jnp.mean(weighted * unit_rows, axis=-1, keepdims=True)
    )


def block_places(blocks, block_len):
    places = blocks[..., None] * block_len + jnp.arange(block_len, dtype=jnp.int32)
    return places.reshape(blocks.shape[:-1] + (2 * block_len,))


def swap_ctx(values, bit):
    number = lax.axis_size("ctx")
    return lax.ppermute(values, "ctx", [(i, i ^ (1 << bit)) for i in range(number)])


def swap_fsdp(values):
    return lax.ppermute(values, "fsdp", [(0, 1), (1, 0)])


def ctx_bit(bit):
    return (lax.axis_index("ctx") >> bit) & 1


def join(mine, other, bit, axis):
    first = jnp.where(bit == 0, mine, other)
    second = jnp.where(bit == 0, other, mine)
    return jnp.concatenate([first, second], axis=axis)


def gather_weight(part):
    rows = part.shape[0]
    quarter = rows // 4
    core, chip = ctx_bit(0), ctx_bit(1)
    piece = lax.dynamic_slice_in_dim(part, (core * 2 + chip) * quarter, quarter, 0)
    piece = swap_fsdp(piece)
    half = join(piece, swap_ctx(piece, 1), chip, 0)
    other = join(half, swap_ctx(half, 0), core, 0)
    return join(part, other, lax.axis_index("fsdp"), 0)


def half_of(values, bit, axis):
    size = values.shape[axis] // 2
    return lax.dynamic_slice_in_dim(values, bit * size, size, axis)


def reduce_grad(grad, lead):
    levels = lax.axis_size("ctx").bit_length() - 1
    order = list(lead) + [k for k in range(levels) if k not in lead]
    rows, columns = grad.shape
    total = grad.reshape(2, rows // 2, columns)
    steps = []
    for level in order:
        if level == "x":
            axis, bit = 0, lax.axis_index("fsdp")
        else:
            bit = ctx_bit(level)
            if total.shape[2] % 256 == 0 or total.shape[1] % 2:
                axis = 2
            else:
                axis = 1
            steps.append((level, bit, axis))
        sent = half_of(total, 1 - bit, axis).astype(jnp.bfloat16)
        arrived = swap_fsdp(sent) if level == "x" else swap_ctx(sent, level)
        total = half_of(total, bit, axis).astype(jnp.float32) + arrived.astype(jnp.float32)
    total = lax.reduce_precision(total, 8, 7).astype(jnp.bfloat16)
    for level, bit, axis in reversed(steps):
        total = join(total, swap_ctx(total, level), bit, axis)
    return total[0].astype(jnp.float32)


def scatter_rows(terms):
    devices = lax.axis_size("ctx")
    seqs, total_rows, width = terms.shape
    rows = total_rows // devices
    total = terms
    count = devices
    for level in range(devices.bit_length() - 1):
        bit = ctx_bit(level)
        count //= 2
        total = total.reshape(seqs, count, 2, rows, width)
        sent = lax.dynamic_index_in_dim(total, 1 - bit, 2, keepdims=False)
        kept = lax.dynamic_index_in_dim(total, bit, 2, keepdims=False)
        arrived = swap_ctx(sent.astype(jnp.bfloat16), level)
        total = kept.astype(jnp.float32) + arrived.astype(jnp.float32)
    return total.reshape(seqs * rows, width)


GROUPS = H // KVH
NT = (((1,), (1,)), ((), ()))
TN = (((0,), (0,)), ((), ()))
NN = (((1,), (0,)), ((), ()))


def dot(left, right, dims):
    return lax.dot_general(left, right, dims, preferred_element_type=jnp.float32)


def group_rows(ref, group):
    return jnp.concatenate(
        [ref[0, :, h * HD : (h + 1) * HD] for h in range(group * GROUPS, (group + 1) * GROUPS)],
        axis=0,
    )


def put_rows(ref, group, values):
    rows = values.shape[0] // GROUPS
    for g in range(GROUPS):
        h = group * GROUPS + g
        ref[0, :, h * HD : (h + 1) * HD] = values[g * rows : (g + 1) * rows]


def forward_kernel(q_ref, kv_ref, qp_ref, kp_ref, out_ref, lse_ref, max_s, sum_s, acc_s):
    step = pl.program_id(1)

    @pl.when(step == 0)
    def _():
        max_s[...] = jnp.full(max_s.shape, MASKED, jnp.float32)
        sum_s[...] = jnp.zeros(sum_s.shape, jnp.float32)
        acc_s[...] = jnp.zeros(acc_s.shape, jnp.float32)

    allowed = kp_ref[0] <= qp_ref[0]
    for j in range(KVH):
        query = group_rows(q_ref, j)
        key = kv_ref[0, :, j * HD : (j + 1) * HD]
        value = kv_ref[0, :, (KVH + j) * HD : (KVH + j + 1) * HD]
        scores = jnp.where(allowed, dot(key, query, NT), MASKED)
        top = jnp.maximum(max_s[j], jnp.max(scores, axis=0, keepdims=True))
        probs = jnp.exp(scores - top)
        scale = jnp.exp(max_s[j] - top)
        sum_s[j] = sum_s[j] * scale + jnp.sum(probs, axis=0, keepdims=True)
        acc_s[j] = acc_s[j] * scale + dot(value, probs.astype(jnp.bfloat16), TN)
        max_s[j] = top

    @pl.when(step == pl.num_programs(1) - 1)
    def _():
        for j in range(KVH):
            put_rows(out_ref, j, (acc_s[j] / sum_s[j]).T)
            lse_ref[0, j] = max_s[j] + jnp.log(sum_s[j])


def backward_kernel(
    q_ref, kv_ref, qp_ref, kp_ref, do_ref, out_ref, lse_ref, dq_ref, dkv_ref, dq_s
):
    step = pl.program_id(1)

    @pl.when(step == 0)
    def _():
        dq_s[...] = jnp.zeros(dq_s.shape, jnp.float32)

    allowed = kp_ref[0] <= qp_ref[0]
    for j in range(KVH):
        query = group_rows(q_ref, j)
        grad = group_rows(do_ref, j)
        key = kv_ref[0, :, j * HD : (j + 1) * HD]
        value = kv_ref[0, :, (KVH + j) * HD : (KVH + j + 1) * HD]
        product = grad.astype(jnp.float32) * group_rows(out_ref, j)
        delta = lax.dot_general(
            jnp.ones((8, HD), jnp.float32), product, NT,
            precision=lax.Precision.HIGHEST, preferred_element_type=jnp.float32,
        )[0:1]
        scores = jnp.where(allowed, dot(key, query, NT), MASKED)
        probs = jnp.exp(scores - lse_ref[0, j])
        grad_probs = dot(value, grad, NT)
        grad_scores = (probs * (grad_probs - delta)).astype(jnp.bfloat16)
        dq_s[j] += dot(key, grad_scores, TN)
        dkv_ref[0, :, j * HD : (j + 1) * HD] = dot(grad_scores, query, NN).astype(jnp.bfloat16)
        dkv_ref[0, :, (KVH + j) * HD : (KVH + j + 1) * HD] = dot(
            probs.astype(jnp.bfloat16), grad, NN
        ).astype(jnp.bfloat16)

    @pl.when(step == pl.num_programs(1) - 1)
    def _():
        for j in range(KVH):
            put_rows(dq_ref, j, (dq_s[j] * HD ** (-0.5)).T)


def attention_specs(seqs, rows, keys):
    chunk = min(keys, 2048)
    row = lambda width: pl.BlockSpec((1, rows, width), lambda s, c: (s, 0, 0))
    per_key = lambda width: pl.BlockSpec((1, chunk, width), lambda s, c: (s, c, 0))
    stat = pl.BlockSpec((1, KVH, 1, GROUPS * rows), lambda s, c: (s, 0, 0, 0))
    query_place = pl.BlockSpec((1, 1, GROUPS * rows), lambda s, c: (s, 0, 0))
    params = pltpu.CompilerParams(
        dimension_semantics=("arbitrary", "arbitrary"), vmem_limit_bytes=48 * 1024 * 1024
    )
    return (seqs, keys // chunk), row, per_key, stat, query_place, params


def attend_forward(query, key_value, query_places, key_places):
    seqs, rows, width = query.shape
    keys = key_value.shape[1]
    grid, row, per_key, stat, query_place, params = attention_specs(seqs, rows, keys)
    wide = GROUPS * rows
    return pl.pallas_call(
        forward_kernel,
        grid=grid,
        in_specs=[row(width), per_key(2 * KVH * HD), query_place, per_key(1)],
        out_specs=[row(width), stat],
        out_shape=[
            jax.ShapeDtypeStruct((seqs, rows, width), jnp.float32),
            jax.ShapeDtypeStruct((seqs, KVH, 1, wide), jnp.float32),
        ],
        scratch_shapes=[
            pltpu.VMEM((KVH, 1, wide), jnp.float32),
            pltpu.VMEM((KVH, 1, wide), jnp.float32),
            pltpu.VMEM((KVH, HD, wide), jnp.float32),
        ],
        cost_estimate=pl.CostEstimate(
            flops=seqs * H * rows * keys * 1000, bytes_accessed=2**23, transcendentals=0
        ),
        compiler_params=params,
        name="attend_forward",
    )(query, key_value, query_places, key_places)


def attend_backward(query, key_value, query_places, key_places, grad, out, log_total):
    seqs, rows, width = query.shape
    keys = key_value.shape[1]
    grid, row, per_key, stat, query_place, params = attention_specs(seqs, rows, keys)
    wide = GROUPS * rows
    both = 2 * KVH * HD
    return pl.pallas_call(
        backward_kernel,
        grid=grid,
        in_specs=[
            row(width), per_key(both), query_place, per_key(1), row(width), row(width), stat,
        ],
        out_specs=[row(width), per_key(both)],
        out_shape=[
            jax.ShapeDtypeStruct((seqs, rows, width), jnp.float32),
            jax.ShapeDtypeStruct((seqs, keys, both), jnp.bfloat16),
        ],
        scratch_shapes=[pltpu.VMEM((KVH, HD, wide), jnp.float32)],
        cost_estimate=pl.CostEstimate(
            flops=seqs * H * rows * keys * 2000, bytes_accessed=2**24, transcendentals=0
        ),
        compiler_params=params,
        name="attend_backward",
    )(query, key_value, query_places, key_places, grad, out, log_total)


def on_device(
    tokens,
    cotangent,
    early_block,
    positions,
    norm_gain,
    w_query,
    w_key,
    w_value,
    w_out,
    post_gain,
    w_gate,
    w_up,
    w_down,
):
    f32, bf16 = jnp.float32, jnp.bfloat16
    seq_count, rows_seq, model_width = tokens.shape
    block_len = rows_seq // 2
    devices = lax.axis_size("ctx")
    fsdp_place = lax.axis_index("fsdp")
    gains = jnp.stack([norm_gain, post_gain])
    gains = join(gains, swap_fsdp(gains), fsdp_place, 1).astype(f32)
    gain_one, gain_two = gains[0], gains[1]
    qkv_weight = gather_weight(jnp.concatenate([w_query, w_key, w_value], axis=1))
    out_weight = gather_weight(w_out)
    gate_weight = gather_weight(w_gate)
    up_weight = gather_weight(w_up)
    down_weight = gather_weight(w_down)

    flat_rows = tokens.reshape(-1, model_width).astype(f32)
    scale_one = norm_scale(flat_rows)
    unit_one = flat_rows * scale_one
    normed = (unit_one * gain_one).astype(bf16)
    qkv_raw = jnp.dot(normed, qkv_weight, preferred_element_type=f32)
    cosines, sines = rope_tables(positions.reshape(-1), HD)
    cosines = jnp.tile(cosines, (1, 2 * H))
    sines = jnp.tile(sines, (1, 2 * H))
    query_width, key_width = H * HD, KVH * HD
    key_rot = rotate(qkv_raw[:, query_width : query_width + key_width], cosines, sines)
    own_kv = jnp.concatenate(
        [key_rot.astype(bf16), qkv_raw[:, query_width + key_width :].astype(bf16)], axis=1
    ).reshape(seq_count, rows_seq, 2 * key_width)
    key_value = lax.all_gather(own_kv, "ctx", axis=1, tiled=True)
    query = (
        rotate(qkv_raw[:, :query_width], cosines, sines).astype(bf16) * bf16(HD ** (-0.5))
    ).reshape(seq_count, rows_seq, query_width)
    ctx_place = lax.axis_index("ctx")
    own_early = jnp.sum(
        jnp.where(jnp.arange(devices, dtype=jnp.int32)[None, :] == ctx_place, early_block, 0),
        axis=1,
    )
    own_places = block_places(
        jnp.stack([own_early, 2 * devices - 1 - own_early], axis=-1), block_len
    )
    all_places = block_places(
        jnp.stack([early_block, 2 * devices - 1 - early_block], axis=-1), block_len
    ).reshape(seq_count, devices * rows_seq, 1)
    query_places = jnp.tile(own_places, (1, GROUPS))[:, None, :]
    attended, log_total = attend_forward(query, key_value, query_places, all_places)
    mixed_rows = attended.reshape(-1, query_width).astype(bf16)
    residual = flat_rows + jnp.dot(mixed_rows, out_weight, preferred_element_type=f32)
    scale_two = norm_scale(residual)
    unit_two = residual * scale_two
    normed_two = (unit_two * gain_two).astype(bf16)
    gate_act = jnp.dot(normed_two, gate_weight, preferred_element_type=f32)
    up_act = jnp.dot(normed_two, up_weight, preferred_element_type=f32)
    sigmoid_gate = jax.nn.sigmoid(gate_act)
    hidden = (gate_act * sigmoid_gate * up_act).astype(bf16)
    output = (
        (residual + jnp.dot(hidden, down_weight, preferred_element_type=f32))
        .astype(bf16)
        .reshape(tokens.shape)
    )
    grad_out = cotangent.reshape(-1, model_width)
    grad_hidden = jnp.dot(grad_out, down_weight.T, preferred_element_type=f32)
    grad_up = (grad_hidden * gate_act * sigmoid_gate).astype(bf16)
    grad_gate = (
        grad_hidden * up_act * sigmoid_gate * (1.0 + gate_act * (1.0 - sigmoid_gate))
    ).astype(bf16)
    grad_normed_two = jnp.dot(grad_gate, gate_weight.T, preferred_element_type=f32) + jnp.dot(
        grad_up, up_weight.T, preferred_element_type=f32
    )
    grad_gain_two = jnp.sum(grad_normed_two * unit_two, axis=0)
    grad_residual = grad_out.astype(f32) + norm_back(
        grad_normed_two, unit_two, scale_two, gain_two
    )
    grad_residual_low = grad_residual.astype(bf16)
    grad_mixed = (
        jnp.dot(grad_residual_low, out_weight.T, preferred_element_type=f32)
        .astype(bf16)
        .reshape(seq_count, rows_seq, query_width)
    )
    grad_query, key_value_terms = attend_backward(
        query, key_value, query_places, all_places, grad_mixed, attended, log_total
    )
    owned_down = reduce_grad(
        jnp.dot(hidden.T, grad_out, preferred_element_type=f32).astype(bf16), (0, "x")
    )
    owned_gate = reduce_grad(
        jnp.dot(normed_two.T, grad_gate, preferred_element_type=f32).astype(bf16), (0, 1, "x")
    )
    owned_up = reduce_grad(
        jnp.dot(normed_two.T, grad_up, preferred_element_type=f32).astype(bf16), (0, 2, 1, "x")
    )
    owned_out = reduce_grad(
        jnp.dot(mixed_rows.T, grad_residual_low, preferred_element_type=f32).astype(bf16),
        (0, 2, "x"),
    )
    grad_kv = scatter_rows(key_value_terms)
    grad_qkv = jnp.concatenate(
        [
            rotate(grad_query.reshape(-1, query_width), cosines, -sines).astype(bf16),
            rotate(grad_kv[:, :key_width], cosines, -sines).astype(bf16),
            grad_kv[:, key_width:].astype(bf16),
        ],
        axis=1,
    )
    grad_qkv_w = jnp.dot(normed.T, grad_qkv, preferred_element_type=f32)
    grad_normed = jnp.dot(grad_qkv, qkv_weight.T, preferred_element_type=f32)
    grad_gain_one = jnp.sum(grad_normed * unit_one, axis=0)
    grad_input = (
        (grad_residual + norm_back(grad_normed, unit_one, scale_one, gain_one))
        .astype(bf16)
        .reshape(tokens.shape)
    )
    width = query_width + 2 * key_width
    tail = jnp.concatenate(
        [
            grad_qkv_w.astype(bf16),
            grad_gain_one.astype(bf16)[:, None],
            grad_gain_two.astype(bf16)[:, None],
            jnp.zeros((model_width, (-width - 2) % 128), bf16),
        ],
        axis=1,
    )
    tail = reduce_grad(tail, (0, "x"))
    return (
        output,
        grad_input,
        tail[:, width],
        tail[:, :query_width],
        tail[:, query_width : query_width + key_width],
        tail[:, query_width + key_width : width],
        owned_out,
        tail[:, width + 1],
        owned_gate,
        owned_up,
        owned_down,
    )


def solution(mesh):
    placed = (
        P("fsdp", "ctx", None),
        P("fsdp", "ctx", None),
        P("fsdp", None),
        P("fsdp", "ctx"),
        P("fsdp"),
        P("fsdp", None),
        P("fsdp", None),
        P("fsdp", None),
        P("fsdp", None),
        P("fsdp"),
        P("fsdp", None),
        P("fsdp", None),
        P("fsdp", None),
    )
    return jax.shard_map(
        on_device,
        mesh=mesh,
        in_specs=placed,
        out_specs=(
            P("fsdp", "ctx", None),
            P("fsdp", "ctx", None),
            P("fsdp"),
            P("fsdp", None),
            P("fsdp", None),
            P("fsdp", None),
            P("fsdp", None),
            P("fsdp"),
            P("fsdp", None),
            P("fsdp", None),
            P("fsdp", None),
        ),
        check_vma=False,
    )
```

time: 1610 us -> 592 us (0.37); the launches traced: 1590 us -> 587 us
  waiting for transfers between devices: 672 us -> 193 us
  blocking collectives: 465 us -> 0 us
  local copies, waits for them, and re-layouts: 280 us -> 111 us
  matrix products: 129 us -> 49.8 us
  other arithmetic: 21.7 us -> 98 us
  starting transfers between devices: 1.89 us -> 71.7 us
  Pallas kernels: 0 us -> 47.7 us
    psum x1 -> x0, blocking collectives: 424 us -> none  [on_device(): lax.psum((owned_gain_one, owned_query, owned_key, owned_value, owned_out,...]
    reduce_scatter x9 -> x0, waiting for transfers between devices: 408 us -> none  [the longest x2 131 us: on_device(): lax.psum_scatter(key_terms, 'ctx', scatter_dimension=0, tiled=True)]
    all_gather x7 -> x1, waiting for transfers between devices: 232 us -> 0.01 us  [on_device(): key_value = lax.all_gather(own_kv, 'ctx', axis=1, tiled=True)]
    dynamic_update_slice x16 -> x0, local copies, waits for them, and re-layouts: 197 us -> none  [attend_backward(): lax.scan(accumulate, jnp.zeros(query_rows.shape, jnp.float32), (key_block...]
    ppermute x0 -> x65, waiting for transfers between devices: none -> 193 us  [the longest x54 177 us: swap_ctx(): lax.ppermute(values, 'ctx', [(i, i ^ 1 << bit) for i in range(number)])]
    dot_general x49 -> x15, matrix products: 129 us -> 49.8 us  [the longest x1 16 us: on_device(): gate_act = jnp.dot(normed_two, gate_weight, preferred_element_type=f32)]
    ppermute x0 -> x65, starting transfers between devices: none -> 71.7 us  [the longest x54 60.2 us: swap_ctx(): lax.ppermute(values, 'ctx', [(i, i ^ 1 << bit) for i in range(number)])]
    pallas_call x0 -> x2, Pallas kernels: none -> 47.7 us  [the longest x1 29.9 us: attend_backward(): pl.pallas_call(backward_kernel, grid=grid, in_specs=[row(width), per_key(...]
  transfers between devices with their start and end apart: 18 -> 66, of which waited for: 15 -> 28; matrix products, arithmetic and copies ran while one was open for 17% -> 34% of each run, Pallas kernels for 0% -> 5%
where the time goes in v1:
time: 592 us; the launch traced here: 587 us
  waiting for transfers between devices  193 us (33%)
  local copies, waits for them, and re-layouts  111 us (19%)
  other arithmetic  98 us (17%)
  starting transfers between devices  71.7 us (12%)
  matrix products  49.8 us (8%)
  Pallas kernels  47.7 us (8%)
  between operations  16.3 us (3%)
    ppermute x54, waiting for transfers between devices, swap_ctx(): lax.ppermute(values, 'ctx', [(i, i ^ 1 << bit) for i in range(number)])  177 us
    ppermute x54, starting transfers between devices, swap_ctx(): lax.ppermute(values, 'ctx', [(i, i ^ 1 << bit) for i in range(number)])  60.2 us
    select_n x35, other arithmetic, join(): first = jnp.where(bit == 0, mine, other)  42.6 us
    unnamed x216, local copies, waits for them, and re-layouts  30.1 us
    pallas_call x1, Pallas kernels, attend_backward(): pl.pallas_call(backward_kernel, grid=grid, in_specs=[row(width), per_key(...  29.9 us
    pallas_call x1, Pallas kernels, attend_forward(): pl.pallas_call(forward_kernel, grid=grid, in_specs=[row(width), per_key(2...  17.9 us
    add x20, other arithmetic, reduce_grad(): half_of(total, bit, axis).astype(jnp.float32) + arrived.astype(jnp.float32)  17.6 us
    dot_general x1, matrix products, on_device(): gate_act = jnp.dot(normed_two, gate_weight, preferred_element_type=f32)  16 us
  transfers between devices with their start and end apart: 66, of which 28 were waited for; matrix products, arithmetic and copies ran while one was open for 34% of the time, Pallas kernels for 5%

profile of v1, /device:TPU:1, one launch (start us, length us, event | category | flops | bytes accessed | tf_op | source)
XLA Modules:
  0.0 587.1 jit_solution(10934007823859214790)
XLA Ops:
  18.3 3.0 copy.216
  28.1 6.3 %collective-permute-done.2 = bf16[120,1600]{1,0:T(8,128)(2,1)} collective-permute-done((bf16[120,1600]{1,0:T(8,128)(2,1)S(1)}, bf16[120,1600]{1,0:T(8,128)(2,1)}, u32[]{:S(2)}, u32[]{:S(2)}) %collective-permute-start.2) | collective-permute-done | bytes 384032 | tf_op jit(solution)/shard_map/ppermute | solution.py:55
  36.6 3.0 collective-permute-start.3
  52.2 3.5 add.482
  59.2 6.6 %collective-permute-done.5 = bf16[120,960]{1,0:T(8,128)(2,1)S(1)} collective-permute-done((bf16[120,960]{1,0:T(8,128)(2,1)}, bf16[120,960]{1,0:T(8,128)(2,1)S(1)}, u32[]{:S(2)}, u32[]{:S(2)}) %collective-permute-start.5) | collective-permute-done | bytes 230432 | tf_op jit(solution)/shard_map/ppermute | solution.py:55
  76.1 14.7 %collective-permute-done.14 = bf16[320,960]{1,0:T(8,128)(2,1)} collective-permute-done((bf16[320,960]{1,0:T(8,128)(2,1)}, bf16[320,960]{1,0:T(8,128)(2,1)}, u32[]{:S(2)}, u32[]{:S(2)}) %collective-permute-start.14) | collective-permute-done | bytes 614432 | tf_op jit(solution)/shard_map/ppermute | solution.py:55
  94.5 2.4 copy.213
  98.8 15.2 %collective-permute-done.11 = bf16[120,2560]{1,0:T(8,128)(2,1)} collective-permute-done((bf16[120,2560]{1,0:T(8,128)(2,1)}, bf16[120,2560]{1,0:T(8,128)(2,1)}, u32[]{:S(2)}, u32[]{:S(2)}) %collective-permute-start.11) | collective-permute-done | bytes 614432 | tf_op jit(solution)/shard_map/ppermute | solution.py:55
  114.0 13.2 %collective-permute-done.8 = bf16[120,2560]{1,0:T(8,128)(2,1)} collective-permute-done((bf16[120,2560]{1,0:T(8,128)(2,1)}, bf16[120,2560]{1,0:T(8,128)(2,1)}, u32[]{:S(2)}, u32[]{:S(2)}) %collective-permute-start.8) | collective-permute-done | bytes 614432 | tf_op jit(solution)/shard_map/ppermute | solution.py:55
  134.7 2.4 copy.214
  137.1 2.5 broadcast_select_fusion.11
  141.4 6.2 %convolution_bitcast_fusion = f32[256,2560]{1,0:T(8,128)} fusion(bf16[1280,960]{1,0:T(8,128)(2,1)S(1)} %get-tuple-element.106, bf16[1280,960]{1,0:T(8,128)(2,1)S(1)} %get-tuple-element.105, bf16[2,128,960]{1,2,0:T(8,128)(2,1)S(1)} %copy-done), kind=kOutput, calls=%fused_computation.10 | convolution fusion | flops 1268121600 | bytes 8028160 | tf_op jit(solution)/shard_map/dot_general | solution.py:358
  151.5 3.2 broadcast_select_fusion.3
  154.7 3.1 broadcast_select_fusion.5
  157.8 17.9 %attend_forward.1 = (f32[2,128,960]{2,1,0:T(8,128)S(1)}, f32[2,5,1,384]{3,2,1,0:T(1,128)S(1)}) custom-call(bf16[2,128,960]{2,1,0:T(8,128)(2,1)S(1)} %bitcast.145, bf16[2,2048,640]{2,1,0:T(8,128)(2,1)} %all-gather.2.cloned.1.call-done.kv_ref, s32[2,1,384]{2,1,0:T(1,128)S(1)} %tile.31.qp_ref, s32[2,2048,1]{2,1,0:T(8,128)S(1)} %broadcast_add_fusion.kp_ref), custom_call_target="tpu_custom_call" | custom-call | flops 7864320000 | bytes 8388608 | tf_op jit(solution)/shard_map/attend_forward/pallas_call | solution.py:236
  182.3 16.0 %multiply_convert_fusion.1 = (bf16[256,2560]{1,0:T(8,128)(2,1)S(1)}, bf16[256,2560]{1,0:T(8,128)(2,1)}, bf16[256,2560]{1,0:T(8,128)(2,1)S(1)}) fusion(f32[256,2560]{1,0:T(8,128)S(1)} %copy-done.91, f32[256,2560]{1,0:T(8,128)S(1)} %fusion.2, bf16[256,960]{0,1:T(8,128)(2,1)S(1)} %multiply_convert_fusion.3, bf16[480,2560]{1,0:T(8,128)(2,1)S(1)} %copy-done.55, ...), kind=kOutput, calls=%fused_computation.28 | convolution fusion | flops 1278607360 | bytes 14581760 | tf_op jit(solution)/shard_map/dot_general | solution.py:348
  206.5 3.7 convolution_convert_fusion.2
  214.0 3.4 constant_dynamic-slice_fusion.2
  217.5 29.9 %attend_backward.1 = (f32[2,128,960]{2,1,0:T(8,128)S(1)}, bf16[2,2048,640]{2,1,0:T(8,128)(2,1)}) custom-call(bf16[2,128,960]{2,1,0:T(8,128)(2,1)S(1)} %bitcast.146, bf16[2,2048,640]{2,1,0:T(8,128)(2,1)} %all-gather.2.cloned.1.call-done.kv_ref, s32[2,1,384]{2,1,0:T(1,128)S(1)} %tile.31.qp_ref, s32[2,2048,1]{2,1,0:T(8,128)S(1)} %broadcast_add_fusion.kp_ref, ...), custom_call_target="tpu_custom_call" | custom-call | flops 15728640000 | bytes 16777216 | tf_op jit(solution)/shard_map/attend_backward/pallas_call | solution.py:264
  250.1 2.4 fusion.15
  252.6 8.0 %collective-permute-done.30 = bf16[2,120,960]{2,1,0:T(8,128)(2,1)S(1)} collective-permute-done((bf16[2,120,960]{2,1,0:T(8,128)(2,1)S(1)}, bf16[2,120,960]{2,1,0:T(8,128)(2,1)S(1)}, u32[]{:S(2)}, u32[]{:S(2)}) %collective-permute-start.30) | collective-permute-done | bytes 460832 | tf_op jit(solution)/shard_map/ppermute | solution.py:55
  263.7 3.3 collective-permute-done.31
  268.6 3.7 convolution_convert_fusion
  277.3 2.8 collective-permute-start.16
  282.3 2.7 collective-permute-start.47
  285.0 7.9 %copy.231 = bf16[2560,960]{1,0:T(8,128)(2,1)} copy(bf16[2560,960]{0,1:T(8,128)(2,1)} %convolution_convert_fusion) | data formatting | bytes 9830400 | tf_op jit(solution)/shard_map/convert_element_type | solution.py:380
  294.0 3.5 constant_dynamic-slice_fusion
  297.4 4.3 copy.232
  307.3 3.9 collective-permute-done.36
  314.0 3.0 convert_add_fusion.3
  318.8 2.4 convert_add_fusion.2
  325.2 3.0 copy.233
  328.2 2.9 convert_add_fusion.1
  336.5 3.2 convert_add_fusion
  341.7 2.9 broadcast_select_fusion.39
  355.4 7.8 %collective-permute-done.57 = bf16[1,640,960]{1,2,0:T(8,128)(2,1)} collective-permute-done((bf16[1,640,960]{1,2,0:T(8,128)(2,1)}, bf16[1,640,960]{1,2,0:T(8,128)(2,1)}, u32[]{:S(2)}, u32[]{:S(2)}) %collective-permute-start.57) | collective-permute-done | bytes 1228832 | tf_op jit(solution)/shard_map/ppermute | solution.py:59
  368.0 6.9 %collective-permute-done.17 = bf16[2,4,128,640]{3,2,1,0:T(8,128)(2,1)} collective-permute-done((bf16[2,4,128,640]{3,2,1,0:T(8,128)(2,1)}, bf16[2,4,128,640]{3,2,1,0:T(8,128)(2,1)}, u32[]{:S(2)}, u32[]{:S(2)}) %collective-permute-start.17) | collective-permute-done | bytes 1310752 | tf_op jit(solution)/shard_map/ppermute | solution.py:55
  378.3 9.7 %collective-permute-done.49 = bf16[2,240,640]{2,1,0:T(8,128)(2,1)} collective-permute-done((bf16[2,240,640]{2,1,0:T(8,128)(2,1)}, bf16[2,240,640]{2,1,0:T(8,128)(2,1)}, u32[]{:S(2)}, u32[]{:S(2)}) %collective-permute-start.49) | collective-permute-done | bytes 614432 | tf_op jit(solution)/shard_map/ppermute | solution.py:55
  390.5 11.4 %collective-permute-done.58 = bf16[1,320,960]{2,1,0:T(8,128)(2,1)S(1)} collective-permute-done((bf16[1,320,960]{2,1,0:T(8,128)(2,1)S(1)}, bf16[1,320,960]{2,1,0:T(8,128)(2,1)S(1)}, u32[]{:S(2)}, u32[]{:S(2)}) %collective-permute-start.58) | collective-permute-done | bytes 614432 | tf_op jit(solution)/shard_map/ppermute | solution.py:55
  403.8 2.4 collective-permute-start.42
  406.4 7.8 %collective-permute-done.59 = bf16[1,160,960]{2,1,0:T(8,128)(2,1)S(1)} collective-permute-done((bf16[1,160,960]{2,1,0:T(8,128)(2,1)S(1)}, bf16[1,160,960]{2,1,0:T(8,128)(2,1)S(1)}, u32[]{:S(2)}, u32[]{:S(2)}) %collective-permute-start.59) | collective-permute-done | bytes 307232 | tf_op jit(solution)/shard_map/ppermute | solution.py:55
  414.4 2.5 collective-permute-start.60
  416.9 15.7 %collective-permute-done.42 = bf16[1,120,640]{2,1,0:T(8,128)(2,1)S(1)} collective-permute-done((bf16[1,120,640]{2,1,0:T(8,128)(2,1)S(1)}, bf16[1,120,640]{2,1,0:T(8,128)(2,1)S(1)}, u32[]{:S(2)}, u32[]{:S(2)}) %collective-permute-start.42) | collective-permute-done | bytes 153632 | tf_op jit(solution)/shard_map/ppermute | solution.py:55
  432.7 4.8 collective-permute-done.51
  437.7 10.1 %collective-permute-done.60 = bf16[1,80,960]{2,1,0:T(8,128)(2,1)S(1)} collective-permute-done((bf16[1,80,960]{2,1,0:T(8,128)(2,1)S(1)}, bf16[1,80,960]{2,1,0:T(8,128)(2,1)S(1)}, u32[]{:S(2)}, u32[]{:S(2)}) %collective-permute-start.60) | collective-permute-done | bytes 153632 | tf_op jit(solution)/shard_map/ppermute | solution.py:55
  448.5 4.3 collective-permute-done.43
  453.7 2.4 collective-permute-done.52
  465.3 2.8 multiply_reduce_fusion.1
  468.1 2.8 convolution_convert_fusion.3
  471.4 6.6 %concatenate.183 = bf16[2,480,1664]{2,1,0:T(8,128)(2,1)} concatenate(bf16[2,480,1600]{2,1,0:T(8,128)(2,1)} %bitcast.176, bf16[2,480,1]{2,1,0:T(8,128)(2,1)S(1)} %convert_element_type.459, bf16[2,480,1]{2,1,0:T(8,128)(2,1)S(1)} %copy-done.74, bf16[2,480,62]{2,1,0:T(8,128)(2,1)S(1)} %broadcast_in_dim.62), dimensions={2} | concatenate | bytes 6389760 | tf_op jit(solution)/shard_map/concatenate | solution.py:410
  479.7 4.8 collective-permute-start.20
  496.1 7.4 %collective-permute-done.45 = bf16[1,480,640]{2,1,0:T(8,128)(2,1)S(1)} collective-permute-done((bf16[1,480,640]{2,1,0:T(8,128)(2,1)S(1)}, bf16[1,480,640]{2,1,0:T(8,128)(2,1)S(1)}, u32[]{:S(2)}, u32[]{:S(2)}) %collective-permute-start.45) | collective-permute-done | bytes 614432 | tf_op jit(solution)/shard_map/ppermute | solution.py:55
  506.3 4.4 collective-permute-done.21
  514.9 11.2 %collective-permute-done.22 = bf16[1,120,1664]{2,1,0:T(8,128)(2,1)S(1)} collective-permute-done((bf16[1,120,1664]{2,1,0:T(8,128)(2,1)S(1)}, bf16[1,120,1664]{2,1,0:T(8,128)(2,1)S(1)}, u32[]{:S(2)}, u32[]{:S(2)}) %collective-permute-start.22) | collective-permute-done | bytes 399392 | tf_op jit(solution)/shard_map/ppermute | solution.py:55
  529.0 2.4 copy.236
  534.0 3.5 broadcast_select_fusion.15
  537.5 2.4 copy.237
  544.5 3.3 collective-permute-done.25
  547.9 2.9 fusion.5
  550.8 5.8 copy.243
  559.6 6.6 %collective-permute-done.27 = bf16[1,120,1664]{2,1,0:T(8,128)(2,1)S(1)} collective-permute-done((bf16[1,120,1664]{2,1,0:T(8,128)(2,1)S(1)}, bf16[1,120,1664]{2,1,0:T(8,128)(2,1)S(1)}, u32[]{:S(2)}, u32[]{:S(2)}) %collective-permute-start.27) | collective-permute-done | bytes 399392 | tf_op jit(solution)/shard_map/ppermute | solution.py:55
  566.4 2.4 collective-permute-start.28
  568.8 2.9 fusion.6
  571.7 2.9 fusion.7
  (506 shorter events, 193.7 us)
Async XLA Ops:
  7.2 150.6 %all-gather.2.cloned.1.call-start = ((), (), s32[]{:S(2)}) async-start(), calls=%async_computation | async-start | bytes 5570560 | tf_op jit(solution)/shard_map/all_gather | solution.py:326
  13.0 12.7 %collective-permute-start.1 = (bf16[120,1600]{1,0:T(8,128)(2,1)}, bf16[120,1600]{1,0:T(8,128)(2,1)S(1)}, u32[]{:S(2)}, u32[]{:S(2)}) collective-permute-start(bf16[120,1600]{1,0:T(8,128)(2,1)} %constant_dynamic-slice_fusion.9), channel_id=1, source_target_pairs={{0,1},{1,0},{2,3},{3,2},{4,5},{5,4},{6,7},{7,6},{8,9},{9,8},{10,11... | collective-permute-start | bytes 1152008 | tf_op jit(solution)/shard_map/ppermute | solution.py:59
  15.1 24.6 %collective-permute-start = (bf16[2,480]{1,0:T(2,128)(2,1)S(1)}, bf16[2,480]{1,0:T(2,128)(2,1)S(1)}, u32[]{:S(2)}, u32[]{:S(2)}) collective-permute-start(bf16[2,480]{1,0:T(2,128)(2,1)S(1)} %pad_maximum_fusion.52), channel_id=1, source_target_pairs={{0,1},{1,0},{2,3},{3,2},{4,5},{5,4},{6,7},{7,6},{8,9},{9,8},{10,11... | collective-permute-start | bytes 5768 | tf_op jit(solution)/shard_map/ppermute | solution.py:59
  16.8 38.9 %collective-permute-start.4 = (bf16[120,960]{1,0:T(8,128)(2,1)}, bf16[120,960]{1,0:T(8,128)(2,1)}, u32[]{:S(2)}, u32[]{:S(2)}) collective-permute-start(bf16[120,960]{1,0:T(8,128)(2,1)} %constant_dynamic-slice_fusion.8), channel_id=1, source_target_pairs={{0,1},{1,0},{2,3},{3,2},{4,5},{5,4},{6,7},{7,6},{8,9},{9,8},{10,11... | collective-permute-start | bytes 691208 | tf_op jit(solution)/shard_map/ppermute | solution.py:59
  22.3 47.8 %collective-permute-start.13 = (bf16[320,960]{1,0:T(8,128)(2,1)}, bf16[320,960]{1,0:T(8,128)(2,1)}, u32[]{:S(2)}, u32[]{:S(2)}) collective-permute-start(bf16[320,960]{1,0:T(8,128)(2,1)} %constant_dynamic-slice_fusion.5), channel_id=1, source_target_pairs={{0,1},{1,0},{2,3},{3,2},{4,5},{5,4},{6,7},{7,6},{8,9},{9,8},{10,11... | collective-permute-start | bytes 1843208 | tf_op jit(solution)/shard_map/ppermute | solution.py:59
  24.3 47.2 %collective-permute-start.10 = (bf16[120,2560]{1,0:T(8,128)(2,1)}, bf16[120,2560]{1,0:T(8,128)(2,1)}, u32[]{:S(2)}, u32[]{:S(2)}) collective-permute-start(bf16[120,2560]{1,0:T(8,128)(2,1)} %constant_dynamic-slice_fusion.6), channel_id=1, source_target_pairs={{0,1},{1,0},{2,3},{3,2},{4,5},{5,4},{6,7},{7,6},{8,9},{9,8},{10,11... | collective-permute-start | bytes 1843208 | tf_op jit(solution)/shard_map/ppermute | solution.py:59
  25.7 8.8 %collective-permute-start.2 = (bf16[120,1600]{1,0:T(8,128)(2,1)S(1)}, bf16[120,1600]{1,0:T(8,128)(2,1)}, u32[]{:S(2)}, u32[]{:S(2)}) collective-permute-start(bf16[120,1600]{1,0:T(8,128)(2,1)S(1)} %collective-permute-done.1), channel_id=1, source_target_pairs={{0,4},{2,6},{4,0},{6,2},{8,12},{10,14},{12,8},{14,10},{16,20},{18,... | collective-permute-start | bytes 1152008 | tf_op jit(solution)/shard_map/ppermute | solution.py:55
  51.8 19.9 %collective-permute-start.7 = (bf16[120,2560]{1,0:T(8,128)(2,1)}, bf16[120,2560]{1,0:T(8,128)(2,1)}, u32[]{:S(2)}, u32[]{:S(2)}) collective-permute-start(bf16[120,2560]{1,0:T(8,128)(2,1)} %constant_dynamic-slice_fusion.7), channel_id=1, source_target_pairs={{0,1},{1,0},{2,3},{3,2},{4,5},{5,4},{6,7},{7,6},{8,9},{9,8},{10,11... | collective-permute-start | bytes 1843208 | tf_op jit(solution)/shard_map/ppermute | solution.py:59
  55.8 10.0 %collective-permute-start.5 = (bf16[120,960]{1,0:T(8,128)(2,1)}, bf16[120,960]{1,0:T(8,128)(2,1)S(1)}, u32[]{:S(2)}, u32[]{:S(2)}) collective-permute-start(bf16[120,960]{1,0:T(8,128)(2,1)} %collective-permute-done.4), channel_id=1, source_target_pairs={{0,4},{2,6},{4,0},{6,2},{8,12},{10,14},{12,8},{14,10},{16,20},{18,... | collective-permute-start | bytes 691208 | tf_op jit(solution)/shard_map/ppermute | solution.py:55
  67.6 5.5 collective-permute-start.6
  70.1 20.8 %collective-permute-start.14 = (bf16[320,960]{1,0:T(8,128)(2,1)}, bf16[320,960]{1,0:T(8,128)(2,1)}, u32[]{:S(2)}, u32[]{:S(2)}) collective-permute-start(bf16[320,960]{1,0:T(8,128)(2,1)} %collective-permute-done.13), channel_id=1, source_target_pairs={{0,4},{2,6},{4,0},{6,2},{8,12},{10,14},{12,8},{14,10},{16,20},{18,... | collective-permute-start | bytes 1843208 | tf_op jit(solution)/shard_map/ppermute | solution.py:55
  71.5 42.5 %collective-permute-start.11 = (bf16[120,2560]{1,0:T(8,128)(2,1)}, bf16[120,2560]{1,0:T(8,128)(2,1)}, u32[]{:S(2)}, u32[]{:S(2)}) collective-permute-start(bf16[120,2560]{1,0:T(8,128)(2,1)} %collective-permute-done.10), channel_id=1, source_target_pairs={{0,4},{2,6},{4,0},{6,2},{8,12},{10,14},{12,8},{14,10},{16,20},{18,... | collective-permute-start | bytes 1843208 | tf_op jit(solution)/shard_map/ppermute | solution.py:55
  71.7 55.5 %collective-permute-start.8 = (bf16[120,2560]{1,0:T(8,128)(2,1)}, bf16[120,2560]{1,0:T(8,128)(2,1)}, u32[]{:S(2)}, u32[]{:S(2)}) collective-permute-start(bf16[120,2560]{1,0:T(8,128)(2,1)} %collective-permute-done.7), channel_id=1, source_target_pairs={{0,4},{2,6},{4,0},{6,2},{8,12},{10,14},{12,8},{14,10},{16,20},{18,... | collective-permute-start | bytes 1843208 | tf_op jit(solution)/shard_map/ppermute | solution.py:55
  96.9 37.8 %collective-permute-start.15 = (bf16[640,960]{0,1:T(8,128)(2,1)}, bf16[640,960]{0,1:T(8,128)(2,1)}, u32[]{:S(2)}, u32[]{:S(2)}) collective-permute-start(bf16[640,960]{0,1:T(8,128)(2,1)} %copy.213), channel_id=1, source_target_pairs={{0,2},{2,0},{4,6},{6,4},{8,10},{10,8},{12,14},{14,12},{16,18},{18,... | collective-permute-start | bytes 3686408 | tf_op jit(solution)/shard_map/ppermute | solution.py:55
  130.1 17.5 %collective-permute-start.12 = (bf16[240,2560]{1,0:T(8,128)(2,1)}, bf16[240,2560]{1,0:T(8,128)(2,1)}, u32[]{:S(2)}, u32[]{:S(2)}) collective-permute-start(bf16[240,2560]{1,0:T(8,128)(2,1)} %pad_maximum_fusion.28), channel_id=1, source_target_pairs={{0,2},{2,0},{4,6},{6,4},{8,10},{10,8},{12,14},{14,12},{16,18},{18,... | collective-permute-start | bytes 3686408 | tf_op jit(solution)/shard_map/ppermute | solution.py:55
  132.1 17.4 %collective-permute-start.9 = (bf16[240,2560]{1,0:T(8,128)(2,1)}, bf16[240,2560]{1,0:T(8,128)(2,1)}, u32[]{:S(2)}, u32[]{:S(2)}) collective-permute-start(bf16[240,2560]{1,0:T(8,128)(2,1)} %pad_maximum_fusion.27), channel_id=1, source_target_pairs={{0,2},{2,0},{4,6},{6,4},{8,10},{10,8},{12,14},{14,12},{16,18},{18,... | collective-permute-start | bytes 3686408 | tf_op jit(solution)/shard_map/ppermute | solution.py:55
  213.4 33.9 %collective-permute-start.29 = (bf16[2,240,960]{2,1,0:T(8,128)(2,1)S(1)}, bf16[2,240,960]{2,1,0:T(8,128)(2,1)S(1)}, u32[]{:S(2)}, u32[]{:S(2)}) collective-permute-start(bf16[2,240,960]{2,1,0:T(8,128)(2,1)S(1)} %constant_dynamic-slice_fusion.3), channel_id=1, source_target_pairs={{0,2},{2,0},{4,6},{6,4},{8,10},{10,8},{12,14},{14,12},{16,18},{18,... | collective-permute-start | bytes 2764808 | tf_op jit(solution)/shard_map/ppermute | solution.py:55
  217.4 96.6 %collective-permute-start.38 = (bf16[2,480,1280]{2,1,0:T(8,128)(2,1)}, bf16[2,480,1280]{2,1,0:T(8,128)(2,1)}, u32[]{:S(2)}, u32[]{:S(2)}) collective-permute-start(bf16[2,480,1280]{2,1,0:T(8,128)(2,1)} %constant_dynamic-slice_fusion.2), channel_id=1, source_target_pairs={{0,2},{2,0},{4,6},{6,4},{8,10},{10,8},{12,14},{14,12},{16,18},{18,... | collective-permute-start | bytes 7372808 | tf_op jit(solution)/shard_map/ppermute | solution.py:55
  248.3 12.3 %collective-permute-start.30 = (bf16[2,120,960]{2,1,0:T(8,128)(2,1)S(1)}, bf16[2,120,960]{2,1,0:T(8,128)(2,1)S(1)}, u32[]{:S(2)}, u32[]{:S(2)}) collective-permute-start(bf16[2,120,960]{2,1,0:T(8,128)(2,1)S(1)} %dynamic-slice_convert_fusion.9), channel_id=1, source_target_pairs={{0,8},{2,10},{4,12},{6,14},{8,0},{10,2},{12,4},{14,6},{16,24},{18,... | collective-permute-start | bytes 1382408 | tf_op jit(solution)/shard_map/ppermute | solution.py:55
  260.9 6.2 %collective-permute-start.31 = (bf16[1,120,960]{2,1,0:T(8,128)(2,1)S(1)}, bf16[1,120,960]{2,1,0:T(8,128)(2,1)S(1)}, u32[]{:S(2)}, u32[]{:S(2)}) collective-permute-start(bf16[1,120,960]{2,1,0:T(8,128)(2,1)S(1)} %dynamic-slice_convert_fusion.15), channel_id=1, source_target_pairs={{0,1},{1,0},{2,3},{3,2},{4,5},{5,4},{6,7},{7,6},{8,9},{9,8},{10,11... | collective-permute-start | bytes 691208 | tf_op jit(solution)/shard_map/ppermute | solution.py:59
  272.4 7.7 %collective-permute-start.33 = (bf16[1,30,960]{2,1,0:T(8,128)(2,1)S(1)}, bf16[1,30,960]{2,1,0:T(8,128)(2,1)S(1)}, u32[]{:S(2)}, u32[]{:S(2)}) collective-permute-start(bf16[1,30,960]{2,1,0:T(8,128)(2,1)S(1)} %dynamic-slice_convert_fusion.22), channel_id=1, source_target_pairs={{0,16},{2,18},{4,20},{6,22},{8,24},{10,26},{12,28},{14,30},{16,0},... | collective-permute-start | bytes 172808 | tf_op jit(solution)/shard_map/ppermute | solution.py:55
  277.3 59.2 %collective-permute-start.16 = (bf16[2,8,128,640]{3,2,1,0:T(8,128)(2,1)}, bf16[2,8,128,640]{3,2,1,0:T(8,128)(2,1)}, u32[]{:S(2)}, u32[]{:S(2)}) collective-permute-start(bf16[2,8,128,640]{3,2,1,0:T(8,128)(2,1)} %dynamic-slice_bitcast_fusion), channel_id=1, source_target_pairs={{0,2},{2,0},{4,6},{6,4},{8,10},{10,8},{12,14},{14,12},{16,18},{18,... | collective-permute-start | bytes 7864328 | tf_op jit(solution)/shard_map/ppermute | solution.py:55
  280.2 12.7 %collective-permute-start.34 = (bf16[1,30,960]{2,1,0:T(8,128)(2,1)S(1)}, bf16[1,30,960]{2,1,0:T(8,128)(2,1)S(1)}, u32[]{:S(2)}, u32[]{:S(2)}) collective-permute-start(bf16[1,30,960]{2,1,0:T(8,128)(2,1)S(1)} %reduce-precision_convert_fusion.4), channel_id=1, source_target_pairs={{0,16},{2,18},{4,20},{6,22},{8,24},{10,26},{12,28},{14,30},{16,0},... | collective-permute-start | bytes 172808 | tf_op jit(solution)/shard_map/ppermute | solution.py:55
  282.3 36.6 %collective-permute-start.47 = (bf16[2,480,1280]{2,1,0:T(8,128)(2,1)}, bf16[2,480,1280]{2,1,0:T(8,128)(2,1)}, u32[]{:S(2)}, u32[]{:S(2)}) collective-permute-start(bf16[2,480,1280]{2,1,0:T(8,128)(2,1)} %constant_dynamic-slice_fusion.1), channel_id=1, source_target_pairs={{0,2},{2,0},{4,6},{6,4},{8,10},{10,8},{12,14},{14,12},{16,18},{18,... | collective-permute-start | bytes 7372808 | tf_op jit(solution)/shard_map/ppermute | solution.py:55
  292.9 9.2 %collective-permute-start.35 = (bf16[1,60,960]{2,1,0:T(8,128)(2,1)S(1)}, bf16[1,60,960]{2,1,0:T(8,128)(2,1)S(1)}, u32[]{:S(2)}, u32[]{:S(2)}) collective-permute-start(bf16[1,60,960]{2,1,0:T(8,128)(2,1)S(1)} %pad_maximum_fusion.51), channel_id=1, source_target_pairs={{0,4},{2,6},{4,0},{6,2},{8,12},{10,14},{12,8},{14,10},{16,20},{18,... | collective-permute-start | bytes 345608 | tf_op jit(solution)/shard_map/ppermute | solution.py:55
  301.8 23.5 %collective-permute-start.56 = (bf16[2,640,960]{1,2,0:T(8,128)(2,1)}, bf16[2,640,960]{1,2,0:T(8,128)(2,1)}, u32[]{:S(2)}, u32[]{:S(2)}) collective-permute-start(bf16[2,640,960]{1,2,0:T(8,128)(2,1)} %copy.232), channel_id=1, source_target_pairs={{0,2},{2,0},{4,6},{6,4},{8,10},{10,8},{12,14},{14,12},{16,18},{18,... | collective-permute-start | bytes 7372808 | tf_op jit(solution)/shard_map/ppermute | solution.py:55
  302.9 8.4 %collective-permute-start.36 = (bf16[1,120,960]{2,1,0:T(8,128)(2,1)}, bf16[1,120,960]{2,1,0:T(8,128)(2,1)}, u32[]{:S(2)}, u32[]{:S(2)}) collective-permute-start(bf16[1,120,960]{2,1,0:T(8,128)(2,1)} %pad_maximum_fusion.49), channel_id=1, source_target_pairs={{0,8},{2,10},{4,12},{6,14},{8,0},{10,2},{12,4},{14,6},{16,24},{18,... | collective-permute-start | bytes 691208 | tf_op jit(solution)/shard_map/ppermute | solution.py:55
  313.3 28.4 %collective-permute-start.37 = (bf16[1,240,960]{2,1,0:T(8,128)(2,1)}, bf16[1,240,960]{2,1,0:T(8,128)(2,1)}, u32[]{:S(2)}, u32[]{:S(2)}) collective-permute-start(bf16[1,240,960]{2,1,0:T(8,128)(2,1)} %pad_maximum_fusion.41), channel_id=1, source_target_pairs={{0,2},{2,0},{4,6},{6,4},{8,10},{10,8},{12,14},{14,12},{16,18},{18,... | collective-permute-start | bytes 1382408 | tf_op jit(solution)/shard_map/ppermute | solution.py:55
  318.3 28.4 %collective-permute-start.39 = (bf16[2,480,640]{2,1,0:T(8,128)(2,1)}, bf16[2,480,640]{2,1,0:T(8,128)(2,1)}, u32[]{:S(2)}, u32[]{:S(2)}) collective-permute-start(bf16[2,480,640]{2,1,0:T(8,128)(2,1)} %dynamic-slice_convert_fusion.3), channel_id=1, source_target_pairs={{0,4},{2,6},{4,0},{6,2},{8,12},{10,14},{12,8},{14,10},{16,20},{18,... | collective-permute-start | bytes 3686408 | tf_op jit(solution)/shard_map/ppermute | solution.py:55
  323.9 28.4 %collective-permute-start.48 = (bf16[2,480,640]{2,1,0:T(8,128)(2,1)}, bf16[2,480,640]{2,1,0:T(8,128)(2,1)}, u32[]{:S(2)}, u32[]{:S(2)}) collective-permute-start(bf16[2,480,640]{2,1,0:T(8,128)(2,1)} %dynamic-slice_convert_fusion.2), channel_id=1, source_target_pairs={{0,8},{2,10},{4,12},{6,14},{8,0},{10,2},{12,4},{14,6},{16,24},{18,... | collective-permute-start | bytes 3686408 | tf_op jit(solution)/shard_map/ppermute | solution.py:55
  335.3 28.0 %collective-permute-start.57 = (bf16[1,640,960]{1,2,0:T(8,128)(2,1)}, bf16[1,640,960]{1,2,0:T(8,128)(2,1)}, u32[]{:S(2)}, u32[]{:S(2)}) collective-permute-start(bf16[1,640,960]{1,2,0:T(8,128)(2,1)} %copy.234), channel_id=1, source_target_pairs={{0,1},{1,0},{2,3},{3,2},{4,5},{5,4},{6,7},{7,6},{8,9},{9,8},{10,11... | collective-permute-start | bytes 3686408 | tf_op jit(solution)/shard_map/ppermute | solution.py:59
  341.0 33.9 %collective-permute-start.17 = (bf16[2,4,128,640]{3,2,1,0:T(8,128)(2,1)}, bf16[2,4,128,640]{3,2,1,0:T(8,128)(2,1)}, u32[]{:S(2)}, u32[]{:S(2)}) collective-permute-start(bf16[2,4,128,640]{3,2,1,0:T(8,128)(2,1)} %fusion.13), channel_id=1, source_target_pairs={{0,4},{2,6},{4,0},{6,2},{8,12},{10,14},{12,8},{14,10},{16,20},{18,... | collective-permute-start | bytes 3932168 | tf_op jit(solution)/shard_map/ppermute | solution.py:55
  349.3 28.5 %collective-permute-start.40 = (bf16[1,480,640]{2,1,0:T(8,128)(2,1)}, bf16[1,480,640]{2,1,0:T(8,128)(2,1)S(1)}, u32[]{:S(2)}, u32[]{:S(2)}) collective-permute-start(bf16[1,480,640]{2,1,0:T(8,128)(2,1)} %dynamic-slice_convert_fusion.8), channel_id=1, source_target_pairs={{0,1},{1,0},{2,3},{3,2},{4,5},{5,4},{6,7},{7,6},{8,9},{9,8},{10,11... | collective-permute-start | bytes 1843208 | tf_op jit(solution)/shard_map/ppermute | solution.py:59
  354.8 33.3 %collective-permute-start.49 = (bf16[2,240,640]{2,1,0:T(8,128)(2,1)}, bf16[2,240,640]{2,1,0:T(8,128)(2,1)}, u32[]{:S(2)}, u32[]{:S(2)}) collective-permute-start(bf16[2,240,640]{2,1,0:T(8,128)(2,1)} %dynamic-slice_convert_fusion.7), channel_id=1, source_target_pairs={{0,4},{2,6},{4,0},{6,2},{8,12},{10,14},{12,8},{14,10},{16,20},{18,... | collective-permute-start | bytes 1843208 | tf_op jit(solution)/shard_map/ppermute | solution.py:55
  367.4 34.6 %collective-permute-start.58 = (bf16[1,320,960]{2,1,0:T(8,128)(2,1)S(1)}, bf16[1,320,960]{2,1,0:T(8,128)(2,1)S(1)}, u32[]{:S(2)}, u32[]{:S(2)}) collective-permute-start(bf16[1,320,960]{2,1,0:T(8,128)(2,1)S(1)} %dynamic-slice_convert_fusion.5), channel_id=1, source_target_pairs={{0,4},{2,6},{4,0},{6,2},{8,12},{10,14},{12,8},{14,10},{16,20},{18,... | collective-permute-start | bytes 1843208 | tf_op jit(solution)/shard_map/ppermute | solution.py:55
  376.5 26.9 %collective-permute-start.18 = (bf16[2,2,128,640]{3,2,1,0:T(8,128)(2,1)S(1)}, bf16[2,2,128,640]{3,2,1,0:T(8,128)(2,1)S(1)}, u32[]{:S(2)}, u32[]{:S(2)}) collective-permute-start(bf16[2,2,128,640]{3,2,1,0:T(8,128)(2,1)S(1)} %fusion.26), channel_id=1, source_target_pairs={{0,8},{2,10},{4,12},{6,14},{8,0},{10,2},{12,4},{14,6},{16,24},{18,... | collective-permute-start | bytes 1966088 | tf_op jit(solution)/shard_map/ppermute | solution.py:55
  378.0 25.7 %collective-permute-start.41 = (bf16[1,240,640]{2,1,0:T(8,128)(2,1)S(1)}, bf16[1,240,640]{2,1,0:T(8,128)(2,1)S(1)}, u32[]{:S(2)}, u32[]{:S(2)}) collective-permute-start(bf16[1,240,640]{2,1,0:T(8,128)(2,1)S(1)} %dynamic-slice_convert_fusion.14), channel_id=1, source_target_pairs={{0,8},{2,10},{4,12},{6,14},{8,0},{10,2},{12,4},{14,6},{16,24},{18,... | collective-permute-start | bytes 921608 | tf_op jit(solution)/shard_map/ppermute | solution.py:55
  389.3 17.0 %collective-permute-start.50 = (bf16[1,240,640]{2,1,0:T(8,128)(2,1)S(1)}, bf16[1,240,640]{2,1,0:T(8,128)(2,1)S(1)}, u32[]{:S(2)}, u32[]{:S(2)}) collective-permute-start(bf16[1,240,640]{2,1,0:T(8,128)(2,1)S(1)} %dynamic-slice_convert_fusion.13), channel_id=1, source_target_pairs={{0,1},{1,0},{2,3},{3,2},{4,5},{5,4},{6,7},{7,6},{8,9},{9,8},{10,11... | collective-permute-start | bytes 921608 | tf_op jit(solution)/shard_map/ppermute | solution.py:59
  402.2 12.0 %collective-permute-start.59 = (bf16[1,160,960]{2,1,0:T(8,128)(2,1)S(1)}, bf16[1,160,960]{2,1,0:T(8,128)(2,1)S(1)}, u32[]{:S(2)}, u32[]{:S(2)}) collective-permute-start(bf16[1,160,960]{2,1,0:T(8,128)(2,1)S(1)} %dynamic-slice_convert_fusion.11), channel_id=1, source_target_pairs={{0,8},{2,10},{4,12},{6,14},{8,0},{10,2},{12,4},{14,6},{16,24},{18,... | collective-permute-start | bytes 921608 | tf_op jit(solution)/shard_map/ppermute | solution.py:55
  403.6 53.8 %collective-permute-start.19 = (bf16[2,1,128,640]{3,2,1,0:T(8,128)(2,1)S(1)}, bf16[2,1,128,640]{3,2,1,0:T(8,128)(2,1)S(1)}, u32[]{:S(2)}, u32[]{:S(2)}) collective-permute-start(bf16[2,1,128,640]{3,2,1,0:T(8,128)(2,1)S(1)} %dynamic-slice_convert_fusion.12), channel_id=1, source_target_pairs={{0,16},{2,18},{4,20},{6,22},{8,24},{10,26},{12,28},{14,30},{16,0},... | collective-permute-start | bytes 983048 | tf_op jit(solution)/shard_map/ppermute | solution.py:55
  403.8 28.8 %collective-permute-start.42 = (bf16[1,120,640]{2,1,0:T(8,128)(2,1)S(1)}, bf16[1,120,640]{2,1,0:T(8,128)(2,1)S(1)}, u32[]{:S(2)}, u32[]{:S(2)}) collective-permute-start(bf16[1,120,640]{2,1,0:T(8,128)(2,1)S(1)} %dynamic-slice_convert_fusion.19), channel_id=1, source_target_pairs={{0,16},{2,18},{4,20},{6,22},{8,24},{10,26},{12,28},{14,30},{16,0},... | collective-permute-start | bytes 460808 | tf_op jit(solution)/shard_map/ppermute | solution.py:55
  406.4 31.2 %collective-permute-start.51 = (bf16[1,120,640]{2,1,0:T(8,128)(2,1)S(1)}, bf16[1,120,640]{2,1,0:T(8,128)(2,1)S(1)}, u32[]{:S(2)}, u32[]{:S(2)}) collective-permute-start(bf16[1,120,640]{2,1,0:T(8,128)(2,1)S(1)} %dynamic-slice_convert_fusion.18), channel_id=1, source_target_pairs={{0,16},{2,18},{4,20},{6,22},{8,24},{10,26},{12,28},{14,30},{16,0},... | collective-permute-start | bytes 460808 | tf_op jit(solution)/shard_map/ppermute | solution.py:55
  414.4 33.4 %collective-permute-start.60 = (bf16[1,80,960]{2,1,0:T(8,128)(2,1)S(1)}, bf16[1,80,960]{2,1,0:T(8,128)(2,1)S(1)}, u32[]{:S(2)}, u32[]{:S(2)}) collective-permute-start(bf16[1,80,960]{2,1,0:T(8,128)(2,1)S(1)} %dynamic-slice_convert_fusion.17), channel_id=1, source_target_pairs={{0,16},{2,18},{4,20},{6,22},{8,24},{10,26},{12,28},{14,30},{16,0},... | collective-permute-start | bytes 460808 | tf_op jit(solution)/shard_map/ppermute | solution.py:55
  432.7 20.2 %collective-permute-start.43 = (bf16[1,120,640]{2,1,0:T(8,128)(2,1)S(1)}, bf16[1,120,640]{2,1,0:T(8,128)(2,1)S(1)}, u32[]{:S(2)}, u32[]{:S(2)}) collective-permute-start(bf16[1,120,640]{2,1,0:T(8,128)(2,1)S(1)} %reduce-precision_convert_fusion.2), channel_id=1, source_target_pairs={{0,16},{2,18},{4,20},{6,22},{8,24},{10,26},{12,28},{14,30},{16,0},... | collective-permute-start | bytes 460808 | tf_op jit(solution)/shard_map/ppermute | solution.py:55
  437.6 18.5 %collective-permute-start.52 = (bf16[1,120,640]{2,1,0:T(8,128)(2,1)S(1)}, bf16[1,120,640]{2,1,0:T(8,128)(2,1)S(1)}, u32[]{:S(2)}, u32[]{:S(2)}) collective-permute-start(bf16[1,120,640]{2,1,0:T(8,128)(2,1)S(1)} %reduce-precision_convert_fusion.1), channel_id=1, source_target_pairs={{0,16},{2,18},{4,20},{6,22},{8,24},{10,26},{12,28},{14,30},{16,0},... | collective-permute-start | bytes 460808 | tf_op jit(solution)/shard_map/ppermute | solution.py:55
  448.5 35.9 %collective-permute-start.61 = (bf16[1,80,960]{2,1,0:T(8,128)(2,1)}, bf16[1,80,960]{2,1,0:T(8,128)(2,1)}, u32[]{:S(2)}, u32[]{:S(2)}) collective-permute-start(bf16[1,80,960]{2,1,0:T(8,128)(2,1)} %reduce-precision_convert_fusion), channel_id=1, source_target_pairs={{0,16},{2,18},{4,20},{6,22},{8,24},{10,26},{12,28},{14,30},{16,0},... | collective-permute-start | bytes 460808 | tf_op jit(solution)/shard_map/ppermute | solution.py:55
  453.7 33.0 %collective-permute-start.44 = (bf16[1,240,640]{2,1,0:T(8,128)(2,1)}, bf16[1,240,640]{2,1,0:T(8,128)(2,1)}, u32[]{:S(2)}, u32[]{:S(2)}) collective-permute-start(bf16[1,240,640]{2,1,0:T(8,128)(2,1)} %pad_maximum_fusion.47), channel_id=1, source_target_pairs={{0,8},{2,10},{4,12},{6,14},{8,0},{10,2},{12,4},{14,6},{16,24},{18,... | collective-permute-start | bytes 921608 | tf_op jit(solution)/shard_map/ppermute | solution.py:55
  456.9 32.1 %collective-permute-start.53 = (bf16[1,240,640]{2,1,0:T(8,128)(2,1)}, bf16[1,240,640]{2,1,0:T(8,128)(2,1)}, u32[]{:S(2)}, u32[]{:S(2)}) collective-permute-start(bf16[1,240,640]{2,1,0:T(8,128)(2,1)} %pad_maximum_fusion.48), channel_id=1, source_target_pairs={{0,4},{2,6},{4,0},{6,2},{8,12},{10,14},{12,8},{14,10},{16,20},{18,... | collective-permute-start | bytes 921608 | tf_op jit(solution)/shard_map/ppermute | solution.py:55
  479.7 12.0 %collective-permute-start.20 = (bf16[2,240,1664]{2,1,0:T(8,128)(2,1)S(1)}, bf16[2,240,1664]{2,1,0:T(8,128)(2,1)S(1)}, u32[]{:S(2)}, u32[]{:S(2)}) collective-permute-start(bf16[2,240,1664]{2,1,0:T(8,128)(2,1)S(1)} %constant_dynamic-slice_fusion.4), channel_id=1, source_target_pairs={{0,2},{2,0},{4,6},{6,4},{8,10},{10,8},{12,14},{14,12},{16,18},{18,... | collective-permute-start | bytes 4792328 | tf_op jit(solution)/shard_map/ppermute | solution.py:55
  485.5 9.4 %collective-permute-start.62 = (bf16[1,160,960]{2,1,0:T(8,128)(2,1)S(1)}, bf16[1,160,960]{2,1,0:T(8,128)(2,1)S(1)}, u32[]{:S(2)}, u32[]{:S(2)}) collective-permute-start(bf16[1,160,960]{2,1,0:T(8,128)(2,1)S(1)} %pad_maximum_fusion.46), channel_id=1, source_target_pairs={{0,8},{2,10},{4,12},{6,14},{8,0},{10,2},{12,4},{14,6},{16,24},{18,... | collective-permute-start | bytes 921608 | tf_op jit(solution)/shard_map/ppermute | solution.py:55
  488.0 15.5 %collective-permute-start.45 = (bf16[1,480,640]{2,1,0:T(8,128)(2,1)S(1)}, bf16[1,480,640]{2,1,0:T(8,128)(2,1)S(1)}, u32[]{:S(2)}, u32[]{:S(2)}) collective-permute-start(bf16[1,480,640]{2,1,0:T(8,128)(2,1)S(1)} %pad_maximum_fusion.38), channel_id=1, source_target_pairs={{0,4},{2,6},{4,0},{6,2},{8,12},{10,14},{12,8},{14,10},{16,20},{18,... | collective-permute-start | bytes 1843208 | tf_op jit(solution)/shard_map/ppermute | solution.py:55
  490.2 21.2 %collective-permute-start.54 = (bf16[1,480,640]{2,1,0:T(8,128)(2,1)S(1)}, bf16[1,480,640]{2,1,0:T(8,128)(2,1)S(1)}, u32[]{:S(2)}, u32[]{:S(2)}) collective-permute-start(bf16[1,480,640]{2,1,0:T(8,128)(2,1)S(1)} %pad_maximum_fusion.39), channel_id=1, source_target_pairs={{0,8},{2,10},{4,12},{6,14},{8,0},{10,2},{12,4},{14,6},{16,24},{18,... | collective-permute-start | bytes 1843208 | tf_op jit(solution)/shard_map/ppermute | solution.py:55
  492.1 18.5 %collective-permute-start.21 = (bf16[1,240,1664]{2,1,0:T(8,128)(2,1)S(1)}, bf16[1,240,1664]{2,1,0:T(8,128)(2,1)S(1)}, u32[]{:S(2)}, u32[]{:S(2)}) collective-permute-start(bf16[1,240,1664]{2,1,0:T(8,128)(2,1)S(1)} %dynamic-slice_convert_fusion.4), channel_id=1, source_target_pairs={{0,1},{1,0},{2,3},{3,2},{4,5},{5,4},{6,7},{7,6},{8,9},{9,8},{10,11... | collective-permute-start | bytes 2396168 | tf_op jit(solution)/shard_map/ppermute | solution.py:59
  495.1 32.4 %collective-permute-start.63 = (bf16[1,320,960]{2,1,0:T(8,128)(2,1)S(1)}, bf16[1,320,960]{2,1,0:T(8,128)(2,1)S(1)}, u32[]{:S(2)}, u32[]{:S(2)}) collective-permute-start(bf16[1,320,960]{2,1,0:T(8,128)(2,1)S(1)} %pad_maximum_fusion.37), channel_id=1, source_target_pairs={{0,4},{2,6},{4,0},{6,2},{8,12},{10,14},{12,8},{14,10},{16,20},{18,... | collective-permute-start | bytes 1843208 | tf_op jit(solution)/shard_map/ppermute | solution.py:55
  505.1 29.0 %collective-permute-start.46 = (bf16[1,480,1280]{2,1,0:T(8,128)(2,1)}, bf16[1,480,1280]{2,1,0:T(8,128)(2,1)}, u32[]{:S(2)}, u32[]{:S(2)}) collective-permute-start(bf16[1,480,1280]{2,1,0:T(8,128)(2,1)} %pad_maximum_fusion.29), channel_id=1, source_target_pairs={{0,2},{2,0},{4,6},{6,4},{8,10},{10,8},{12,14},{14,12},{16,18},{18,... | collective-permute-start | bytes 3686408 | tf_op jit(solution)/shard_map/ppermute | solution.py:55
  510.9 15.3 %collective-permute-start.22 = (bf16[1,120,1664]{2,1,0:T(8,128)(2,1)S(1)}, bf16[1,120,1664]{2,1,0:T(8,128)(2,1)S(1)}, u32[]{:S(2)}, u32[]{:S(2)}) collective-permute-start(bf16[1,120,1664]{2,1,0:T(8,128)(2,1)S(1)} %dynamic-slice_convert_fusion.10), channel_id=1, source_target_pairs={{0,4},{2,6},{4,0},{6,2},{8,12},{10,14},{12,8},{14,10},{16,20},{18,... | collective-permute-start | bytes 1198088 | tf_op jit(solution)/shard_map/ppermute | solution.py:55
  512.9 45.0 %collective-permute-start.55 = (bf16[1,480,1280]{2,1,0:T(8,128)(2,1)}, bf16[1,480,1280]{2,1,0:T(8,128)(2,1)}, u32[]{:S(2)}, u32[]{:S(2)}) collective-permute-start(bf16[1,480,1280]{2,1,0:T(8,128)(2,1)} %pad_maximum_fusion.30), channel_id=1, source_target_pairs={{0,2},{2,0},{4,6},{6,4},{8,10},{10,8},{12,14},{14,12},{16,18},{18,... | collective-permute-start | bytes 3686408 | tf_op jit(solution)/shard_map/ppermute | solution.py:55
  526.3 6.5 %collective-permute-start.23 = (bf16[1,60,1664]{2,1,0:T(8,128)(2,1)S(1)}, bf16[1,60,1664]{2,1,0:T(8,128)(2,1)S(1)}, u32[]{:S(2)}, u32[]{:S(2)}) collective-permute-start(bf16[1,60,1664]{2,1,0:T(8,128)(2,1)S(1)} %dynamic-slice_convert_fusion.16), channel_id=1, source_target_pairs={{0,8},{2,10},{4,12},{6,14},{8,0},{10,2},{12,4},{14,6},{16,24},{18,... | collective-permute-start | bytes 599048 | tf_op jit(solution)/shard_map/ppermute | solution.py:55
  531.4 6.1 %collective-permute-start.64 = (bf16[1,640,960]{1,2,0:T(8,128)(2,1)}, bf16[1,640,960]{1,2,0:T(8,128)(2,1)}, u32[]{:S(2)}, u32[]{:S(2)}) collective-permute-start(bf16[1,640,960]{1,2,0:T(8,128)(2,1)} %copy.236), channel_id=1, source_target_pairs={{0,2},{2,0},{4,6},{6,4},{8,10},{10,8},{12,14},{14,12},{16,18},{18,... | collective-permute-start | bytes 3686408 | tf_op jit(solution)/shard_map/ppermute | solution.py:55
  533.9 7.7 %collective-permute-start.24 = (bf16[1,30,1664]{2,1,0:T(8,128)(2,1)S(1)}, bf16[1,30,1664]{2,1,0:T(8,128)(2,1)S(1)}, u32[]{:S(2)}, u32[]{:S(2)}) collective-permute-start(bf16[1,30,1664]{2,1,0:T(8,128)(2,1)S(1)} %dynamic-slice_convert_fusion.21), channel_id=1, source_target_pairs={{0,16},{2,18},{4,20},{6,22},{8,24},{10,26},{12,28},{14,30},{16,0},... | collective-permute-start | bytes 299528 | tf_op jit(solution)/shard_map/ppermute | solution.py:55
  541.6 6.1 %collective-permute-start.25 = (bf16[1,30,1664]{2,1,0:T(8,128)(2,1)S(1)}, bf16[1,30,1664]{2,1,0:T(8,128)(2,1)S(1)}, u32[]{:S(2)}, u32[]{:S(2)}) collective-permute-start(bf16[1,30,1664]{2,1,0:T(8,128)(2,1)S(1)} %reduce-precision_convert_fusion.3), channel_id=1, source_target_pairs={{0,16},{2,18},{4,20},{6,22},{8,24},{10,26},{12,28},{14,30},{16,0},... | collective-permute-start | bytes 299528 | tf_op jit(solution)/shard_map/ppermute | solution.py:55
  547.8 8.8 %collective-permute-start.26 = (bf16[1,60,1664]{2,1,0:T(8,128)(2,1)S(1)}, bf16[1,60,1664]{2,1,0:T(8,128)(2,1)S(1)}, u32[]{:S(2)}, u32[]{:S(2)}) collective-permute-start(bf16[1,60,1664]{2,1,0:T(8,128)(2,1)S(1)} %pad_maximum_fusion.50), channel_id=1, source_target_pairs={{0,8},{2,10},{4,12},{6,14},{8,0},{10,2},{12,4},{14,6},{16,24},{18,... | collective-permute-start | bytes 599048 | tf_op jit(solution)/shard_map/ppermute | solution.py:55
  556.8 9.4 %collective-permute-start.27 = (bf16[1,120,1664]{2,1,0:T(8,128)(2,1)S(1)}, bf16[1,120,1664]{2,1,0:T(8,128)(2,1)S(1)}, u32[]{:S(2)}, u32[]{:S(2)}) collective-permute-start(bf16[1,120,1664]{2,1,0:T(8,128)(2,1)S(1)} %pad_maximum_fusion.42), channel_id=1, source_target_pairs={{0,4},{2,6},{4,0},{6,2},{8,12},{10,14},{12,8},{14,10},{16,20},{18,... | collective-permute-start | bytes 1198088 | tf_op jit(solution)/shard_map/ppermute | solution.py:55
  566.4 8.1 %collective-permute-start.28 = (bf16[1,240,1664]{2,1,0:T(8,128)(2,1)S(1)}, bf16[1,240,1664]{2,1,0:T(8,128)(2,1)S(1)}, u32[]{:S(2)}, u32[]{:S(2)}) collective-permute-start(bf16[1,240,1664]{2,1,0:T(8,128)(2,1)S(1)} %pad_maximum_fusion.36), channel_id=1, source_target_pairs={{0,2},{2,0},{4,6},{6,4},{8,10},{10,8},{12,14},{14,12},{16,18},{18,... | collective-permute-start | bytes 2396168 | tf_op jit(solution)/shard_map/ppermute | solution.py:55
  (104 other events, 782.1 us)
Sparse Core Ops, SparseCore 0:
  49.9 73.4 all-gather.1

commit v2 on v1

--- a/solution.py
+++ b/solution.py
@@ -69,28 +69,39 @@
     return jnp.concatenate([first, second], axis=axis)
 
 
-def gather_weight(part):
+def fetch_quarter(part):
     rows = part.shape[0]
     quarter = rows // 4
     core, chip = ctx_bit(0), ctx_bit(1)
     piece = lax.dynamic_slice_in_dim(part, (core * 2 + chip) * quarter, quarter, 0)
-    piece = swap_fsdp(piece)
+    return swap_fsdp(piece)
+
+
+def share_quarters(part, piece):
+    core, chip = ctx_bit(0), ctx_bit(1)
     half = join(piece, swap_ctx(piece, 1), chip, 0)
     other = join(half, swap_ctx(half, 0), core, 0)
     return join(part, other, lax.axis_index("fsdp"), 0)
 
 
+def after(*values):
+    return lax.optimization_barrier(values)
+
+
 def half_of(values, bit, axis):
     size = values.shape[axis] // 2
     return lax.dynamic_slice_in_dim(values, bit * size, size, axis)
 
 
-def reduce_grad(grad, lead):
-    levels = lax.axis_size("ctx").bit_length() - 1
-    order = list(lead) + [k for k in range(levels) if k not in lead]
-    rows, columns = grad.shape
-    total = grad.reshape(2, rows // 2, columns)
-    steps = []
+def reduce_grad(grad, order):
+    return gather_grad(*halve_grad(*halve_grad(grad, [], (0, "x")), order))
+
+
+def halve_grad(total, steps, order):
+    steps = list(steps)
+    if total.ndim == 2:
+        rows, columns = total.shape
+        total = total.reshape(2, rows // 2, columns)
     for level in order:
         if level == "x":
             axis, bit = 0, lax.axis_index("fsdp")
@@ -104,6 +115,10 @@
         sent = half_of(total, 1 - bit, axis).astype(jnp.bfloat16)
         arrived = swap_fsdp(sent) if level == "x" else swap_ctx(sent, level)
         total = half_of(total, bit, axis).astype(jnp.float32) + arrived.astype(jnp.float32)
+    return total, steps
+
+
+def gather_grad(total, steps):
     total = lax.reduce_precision(total, 8, 7).astype(jnp.bfloat16)
     for level, bit, axis in reversed(steps):
         total = join(total, swap_ctx(total, level), bit, axis)
@@ -248,7 +263,7 @@
             pltpu.VMEM((KVH, HD, wide), jnp.float32),
         ],
         cost_estimate=pl.CostEstimate(
-            flops=seqs * H * rows * keys * 1000, bytes_accessed=2**23, transcendentals=0
+            flops=seqs * H * rows * keys * 2600, bytes_accessed=2**23, transcendentals=0
         ),
         compiler_params=params,
         name="attend_forward",
@@ -274,7 +289,7 @@
         ],
         scratch_shapes=[pltpu.VMEM((KVH, HD, wide), jnp.float32)],
         cost_estimate=pl.CostEstimate(
-            flops=seqs * H * rows * keys * 2000, bytes_accessed=2**24, transcendentals=0
+            flops=seqs * H * rows * keys * 4300, bytes_accessed=2**24, transcendentals=0
         ),
         compiler_params=params,
         name="attend_backward",
@@ -304,11 +319,10 @@
     gains = jnp.stack([norm_gain, post_gain])
     gains = join(gains, swap_fsdp(gains), fsdp_place, 1).astype(f32)
     gain_one, gain_two = gains[0], gains[1]
-    qkv_weight = gather_weight(jnp.concatenate([w_query, w_key, w_value], axis=1))
-    out_weight = gather_weight(w_out)
-    gate_weight = gather_weight(w_gate)
-    up_weight = gather_weight(w_up)
-    down_weight = gather_weight(w_down)
+    qkv_part = jnp.concatenate([w_query, w_key, w_value], axis=1)
+    qkv_weight = share_quarters(qkv_part, fetch_quarter(qkv_part))
+    out_weight = share_quarters(w_out, fetch_quarter(w_out))
+    gate_piece, up_piece, down_piece = (fetch_quarter(w) for w in (w_gate, w_up, w_down))
 
     flat_rows = tokens.reshape(-1, model_width).astype(f32)
     scale_one = norm_scale(flat_rows)
@@ -324,6 +338,12 @@
         [key_rot.astype(bf16), qkv_raw[:, query_width + key_width :].astype(bf16)], axis=1
     ).reshape(seq_count, rows_seq, 2 * key_width)
     key_value = lax.all_gather(own_kv, "ctx", axis=1, tiled=True)
+    key_value, gate_piece, up_piece, down_piece = after(
+        key_value, gate_piece, up_piece, down_piece
+    )
+    gate_weight = share_quarters(w_gate, gate_piece)
+    up_weight = share_quarters(w_up, up_piece)
+    down_weight = share_quarters(w_down, down_piece)
     query = (
         rotate(qkv_raw[:, :query_width], cosines, sines).astype(bf16) * bf16(HD ** (-0.5))
     ).reshape(seq_count, rows_seq, query_width)
@@ -373,23 +393,47 @@
         .astype(bf16)
         .reshape(seq_count, rows_seq, query_width)
     )
-    grad_query, key_value_terms = attend_backward(
-        query, key_value, query_places, all_places, grad_mixed, attended, log_total
-    )
-    owned_down = reduce_grad(
-        jnp.dot(hidden.T, grad_out, preferred_element_type=f32).astype(bf16), (0, "x")
-    )
-    owned_gate = reduce_grad(
-        jnp.dot(normed_two.T, grad_gate, preferred_element_type=f32).astype(bf16), (0, 1, "x")
-    )
-    owned_up = reduce_grad(
-        jnp.dot(normed_two.T, grad_up, preferred_element_type=f32).astype(bf16), (0, 2, 1, "x")
-    )
-    owned_out = reduce_grad(
+    down_sum, down_steps = halve_grad(
+        jnp.dot(hidden.T, grad_out, preferred_element_type=f32).astype(bf16), [], (0,)
+    )
+    gate_sum, gate_steps = halve_grad(
+        jnp.dot(normed_two.T, grad_gate, preferred_element_type=f32).astype(bf16), [], (0,)
+    )
+    grad_mixed, down_sum, gate_sum = after(grad_mixed, down_sum, gate_sum)
+    query_terms, key_value_terms = [], []
+    for sequence in range(seq_count):
+        part = slice(sequence, sequence + 1)
+        one_query, one_key_value = attend_backward(
+            query[part], key_value[part], query_places[part], all_places[part],
+            grad_mixed[part], attended[part], log_total[part],
+        )
+        query_terms.append(one_query)
+        key_value_terms.append(one_key_value)
+        if sequence == 0:
+            down_sum, down_steps = halve_grad(down_sum, down_steps, ("x",))
+            grad_mixed, down_sum = after(grad_mixed, down_sum)
+    grad_query = jnp.concatenate(query_terms)
+    key_value_terms = jnp.concatenate(key_value_terms)
+    levels = range(1, lax.axis_size("ctx").bit_length() - 1)
+    upward = tuple(levels)
+    middle = (2, 1) + tuple(k for k in levels if k > 2)
+    down_sum, down_steps = halve_grad(down_sum, down_steps, (1,))
+    gate_sum, gate_steps = halve_grad(gate_sum, gate_steps, ("x",))
+    up_sum, up_steps = halve_grad(
+        jnp.dot(normed_two.T, grad_up, preferred_element_type=f32).astype(bf16), [], (0, "x")
+    )
+    out_sum, out_steps = halve_grad(
         jnp.dot(mixed_rows.T, grad_residual_low, preferred_element_type=f32).astype(bf16),
-        (0, 2, "x"),
+        [], (0, "x"),
     )
     grad_kv = scatter_rows(key_value_terms)
+    grad_kv, down_sum, gate_sum, up_sum, out_sum = after(
+        grad_kv, down_sum, gate_sum, up_sum, out_sum
+    )
+    owned_down = gather_grad(*halve_grad(down_sum, down_steps, upward[1:]))
+    owned_gate = gather_grad(*halve_grad(gate_sum, gate_steps, middle))
+    owned_up = gather_grad(*halve_grad(up_sum, up_steps, upward))
+    owned_out = gather_grad(*halve_grad(out_sum, out_steps, middle))
     grad_qkv = jnp.concatenate(
         [
             rotate(grad_query.reshape(-1, query_width), cosines, -sines).astype(bf16),
@@ -416,7 +460,7 @@
         ],
         axis=1,
     )
-    tail = reduce_grad(tail, (0, "x"))
+    tail = reduce_grad(tail, upward)
     return (
         output,
         grad_input,

time: 592 us -> 651 us (1.100)
  waiting for transfers between devices: 193 us -> 232 us
  local copies, waits for them, and re-layouts: 111 us -> 139 us
  matrix products: 49.8 us -> 34.3 us
    ppermute x11, waiting for transfers between devices: 15.5 us -> 93.3 us  [swap_fsdp(): return lax.ppermute(values, 'fsdp', [(0, 1), (1, 0)])]
    ppermute x54, waiting for transfers between devices: 177 us -> 139 us  [swap_ctx(): lax.ppermute(values, 'ctx', [(i, i ^ 1 << bit) for i in range(number)])]
    unnamed x216 -> x251, local copies, waits for them, and re-layouts: 30.1 us -> 44.9 us
    slice x1 -> x12, local copies, waits for them, and re-layouts: 0.03 us -> 13 us  [the longest x1 5.34 us: on_device(): key_value[part]]
    dot_general x1, matrix products: 16 us -> 3.63 us  [on_device(): gate_act = jnp.dot(normed_two, gate_weight, preferred_element_type=f32)]
    select_n x35, other arithmetic: 42.6 us -> 31.2 us  [join(): first = jnp.where(bit == 0, mine, other)]
    add x20, other arithmetic: 17.6 us -> 28.4 us  [halve_grad(): half_of(total, bit, axis).astype(jnp.float32) + arrived.astype(jnp.float32)]
    ppermute x54, starting transfers between devices: 60.2 us -> 66.7 us  [swap_ctx(): lax.ppermute(values, 'ctx', [(i, i ^ 1 << bit) for i in range(number)])]
  transfers between devices with their start and end apart: 66 -> 66, of which waited for: 28 -> 30; matrix products, arithmetic and copies ran while one was open for 34% -> 27% of each run, Pallas kernels for 5% -> 5%
where the time goes in v2:
time: 651 us; the launch traced here: 643 us
  waiting for transfers between devices  232 us (36%)
  local copies, waits for them, and re-layouts  139 us (21%)
  other arithmetic  96.3 us (15%)
  starting transfers between devices  77.2 us (12%)
  Pallas kernels  48.2 us (7%)
  matrix products  34.3 us (5%)
  between operations  16.4 us (3%)
    ppermute x54, waiting for transfers between devices, swap_ctx(): lax.ppermute(values, 'ctx', [(i, i ^ 1 << bit) for i in range(number)])  139 us
    ppermute x11, waiting for transfers between devices, swap_fsdp(): return lax.ppermute(values, 'fsdp', [(0, 1), (1, 0)])  93.3 us
    ppermute x54, starting transfers between devices, swap_ctx(): lax.ppermute(values, 'ctx', [(i, i ^ 1 << bit) for i in range(number)])  66.7 us
    unnamed x251, local copies, waits for them, and re-layouts  44.9 us
    select_n x35, other arithmetic, join(): first = jnp.where(bit == 0, mine, other)  31.2 us
    pallas_call x2, Pallas kernels, attend_backward(): pl.pallas_call(backward_kernel, grid=grid, in_specs=[row(width), per_key(...  30.2 us
    add x20, other arithmetic, halve_grad(): half_of(total, bit, axis).astype(jnp.float32) + arrived.astype(jnp.float32)  28.4 us
    pallas_call x1, Pallas kernels, attend_forward(): pl.pallas_call(forward_kernel, grid=grid, in_specs=[row(width), per_key(2...  18 us
  transfers between devices with their start and end apart: 66, of which 30 were waited for; matrix products, arithmetic and copies ran while one was open for 27% of the time, Pallas kernels for 5%

profile of v2, /device:TPU:1, one launch (start us, length us, event | category | flops | bytes accessed | tf_op | source)
XLA Modules:
  0.0 643.2 jit_solution(9140735128239275985)
XLA Ops:
  14.5 8.8 %collective-permute-done.1 = bf16[120,1600]{1,0:T(8,128)(2,1)S(1)} collective-permute-done((bf16[120,1600]{1,0:T(8,128)(2,1)S(1)}, bf16[120,1600]{1,0:T(8,128)(2,1)S(1)}, u32[]{:S(2)}, u32[]{:S(2)}) %collective-permute-start.1) | collective-permute-done | bytes 384032 | tf_op jit(solution)/shard_map/ppermute | solution.py:59
  24.9 8.1 %collective-permute-done.2 = bf16[120,1600]{1,0:T(8,128)(2,1)} collective-permute-done((bf16[120,1600]{1,0:T(8,128)(2,1)S(1)}, bf16[120,1600]{1,0:T(8,128)(2,1)}, u32[]{:S(2)}, u32[]{:S(2)}) %collective-permute-start.2) | collective-permute-done | bytes 384032 | tf_op jit(solution)/shard_map/ppermute | solution.py:55
  62.7 3.1 copy.275
  70.2 3.5 add.505
  73.9 33.6 %collective-permute-done.7 = bf16[120,960]{1,0:T(8,128)(2,1)} collective-permute-done((bf16[120,960]{1,0:T(8,128)(2,1)S(1)}, bf16[120,960]{1,0:T(8,128)(2,1)}, u32[]{:S(2)}, u32[]{:S(2)}) %collective-permute-start.7) | collective-permute-done | bytes 230432 | tf_op jit(solution)/shard_map/ppermute | solution.py:59
  123.9 2.5 copy.314
  126.6 2.5 copy.311
  129.1 2.5 copy.310
  131.6 3.1 fusion.27
  135.6 5.3 fusion.59
  140.9 18.0 %attend_forward.1 = (f32[2,128,960]{2,1,0:T(8,128)S(1)}, f32[2,5,1,384]{3,2,1,0:T(1,128)S(1)}) custom-call(bf16[2,128,960]{2,1,0:T(8,128)(2,1)S(1)} %bitcast.143, bf16[2,2048,640]{2,1,0:T(8,128)(2,1)} %all-gather.2.cloned.1.call-done.kv_ref, s32[2,1,384]{2,1,0:T(1,128)S(1)} %tile.43.qp_ref, s32[2,2048,1]{2,1,0:T(8,128)S(1)} %broadcast_add_fusion.kp_ref), custom_call_target="tpu_custom_call" | custom-call | flops 20447232000 | bytes 8388608 | tf_op jit(solution)/shard_map/attend_forward/pallas_call | solution.py:251
  164.9 10.7 %collective-permute-done.14 = bf16[320,960]{1,0:T(8,128)(2,1)S(1)} collective-permute-done((bf16[320,960]{1,0:T(8,128)(2,1)}, bf16[320,960]{1,0:T(8,128)(2,1)S(1)}, u32[]{:S(2)}, u32[]{:S(2)}) %collective-permute-start.14) | collective-permute-done | bytes 614432 | tf_op jit(solution)/shard_map/ppermute | solution.py:55
  179.7 9.2 %collective-permute-done.12 = bf16[120,2560]{1,0:T(8,128)(2,1)} collective-permute-done((bf16[120,2560]{1,0:T(8,128)(2,1)}, bf16[120,2560]{1,0:T(8,128)(2,1)}, u32[]{:S(2)}, u32[]{:S(2)}) %collective-permute-start.12) | collective-permute-done | bytes 614432 | tf_op jit(solution)/shard_map/ppermute | solution.py:55
  192.8 9.3 %collective-permute-done.10 = bf16[120,2560]{1,0:T(8,128)(2,1)} collective-permute-done((bf16[120,2560]{1,0:T(8,128)(2,1)}, bf16[120,2560]{1,0:T(8,128)(2,1)}, u32[]{:S(2)}, u32[]{:S(2)}) %collective-permute-start.10) | collective-permute-done | bytes 614432 | tf_op jit(solution)/shard_map/ppermute | solution.py:55
  205.5 2.4 copy.282
  208.0 2.5 broadcast_select_fusion.11
  223.9 3.6 multiply_convert_fusion.1
  227.5 2.4 fusion.1
  229.9 3.7 convolution_convert_fusion
  233.6 7.9 %copy.289 = bf16[2560,960]{1,0:T(8,128)(2,1)} copy(bf16[2560,960]{0,1:T(8,128)(2,1)} %convolution_convert_fusion) | data formatting | bytes 9830400 | tf_op jit(solution)/shard_map/convert_element_type | solution.py:397
  243.5 2.7 copy.290
  246.5 3.1 convolution_convert_fusion.2
  258.9 2.9 convolution_convert_fusion.1
  268.5 4.6 copy.291
  273.1 3.9 convert_add_fusion.1
  277.0 6.3 convert_add_fusion.3
  289.5 15.2 %attend_backward.2 = (f32[1,128,960]{2,1,0:T(8,128)S(1)}, bf16[1,2048,640]{2,1,0:T(8,128)(2,1)S(1)}) custom-call(bf16[1,128,960]{2,1,0:T(8,128)(2,1)S(1)} %copy-done.8, bf16[1,2048,640]{2,1,0:T(8,128)(2,1)} %get-tuple-element.134.kv_ref, s32[1,1,384]{2,1,0:T(1,128)S(1)} %tile.40.qp_ref, s32[1,2048,1]{2,1,0:T(8,128)S(1)} %copy-done.3, ...), custom_call_target="tpu_custom_call" | custom-call | flops 16908288000 | bytes 16777216 | tf_op jit(solution)/shard_map/attend_backward/pallas_call | solution.py:279
  304.8 9.1 %collective-permute-done.18 = bf16[1,640,960]{1,2,0:T(8,128)(2,1)} collective-permute-done((bf16[1,640,960]{1,2,0:T(8,128)(2,1)}, bf16[1,640,960]{1,2,0:T(8,128)(2,1)}, u32[]{:S(2)}, u32[]{:S(2)}) %collective-permute-start.18) | collective-permute-done | bytes 1228832 | tf_op jit(solution)/shard_map/ppermute | solution.py:59
  313.9 2.5 copy.294
  316.4 4.5 convert_add_fusion.5
  321.0 14.9 %attend_backward.3 = (f32[1,128,960]{2,1,0:T(8,128)S(1)}, bf16[1,2048,640]{2,1,0:T(8,128)(2,1)S(1)}) custom-call(bf16[1,128,960]{2,1,0:T(8,128)(2,1)S(1)} %get-tuple-element.214.q_ref, bf16[1,2048,640]{2,1,0:T(8,128)(2,1)} %get-tuple-element.135.kv_ref, s32[1,1,384]{2,1,0:T(1,128)S(1)} %tile.42.qp_ref, s32[1,2048,1]{2,1,0:T(8,128)S(1)} %copy-done.2, ...), custom_call_target="tpu_custom_call" | custom-call | flops 16908288000 | bytes 16777216 | tf_op jit(solution)/shard_map/attend_backward/pallas_call | solution.py:279
  345.2 3.9 fusion.15
  351.1 6.0 collective-permute-done.28
  362.4 3.1 convert_add_fusion.2
  365.5 2.4 convert_add_fusion
  371.5 17.4 %collective-permute-done.24 = bf16[1,480,1280]{2,1,0:T(8,128)(2,1)S(1)} collective-permute-done((bf16[1,480,1280]{2,1,0:T(8,128)(2,1)S(1)}, bf16[1,480,1280]{2,1,0:T(8,128)(2,1)S(1)}, u32[]{:S(2)}, u32[]{:S(2)}) %collective-permute-start.24) | collective-permute-done | bytes 1228832 | tf_op jit(solution)/shard_map/ppermute | solution.py:59
  390.6 6.7 %collective-permute-done.20 = bf16[2,4,128,640]{3,2,1,0:T(8,128)(2,1)S(1)} collective-permute-done((bf16[2,4,128,640]{3,2,1,0:T(8,128)(2,1)S(1)}, bf16[2,4,128,640]{3,2,1,0:T(8,128)(2,1)S(1)}, u32[]{:S(2)}, u32[]{:S(2)}) %collective-permute-start.20) | collective-permute-done | bytes 1310752 | tf_op jit(solution)/shard_map/ppermute | solution.py:55
  399.2 16.1 %collective-permute-done.26 = bf16[1,480,1280]{2,1,0:T(8,128)(2,1)S(1)} collective-permute-done((bf16[1,480,1280]{2,1,0:T(8,128)(2,1)S(1)}, bf16[1,480,1280]{2,1,0:T(8,128)(2,1)S(1)}, u32[]{:S(2)}, u32[]{:S(2)}) %collective-permute-start.26) | collective-permute-done | bytes 1228832 | tf_op jit(solution)/shard_map/ppermute | solution.py:59
  421.5 12.3 %collective-permute-done.22 = bf16[2,1,128,640]{3,2,1,0:T(8,128)(2,1)S(1)} collective-permute-done((bf16[2,1,128,640]{3,2,1,0:T(8,128)(2,1)S(1)}, bf16[2,1,128,640]{3,2,1,0:T(8,128)(2,1)S(1)}, u32[]{:S(2)}, u32[]{:S(2)}) %collective-permute-start.22) | collective-permute-done | bytes 327712 | tf_op jit(solution)/shard_map/ppermute | solution.py:55
  438.4 3.5 multiply_reduce_fusion.1
  446.1 5.4 concatenate.191
  466.4 8.2 %collective-permute-done.39 = bf16[1,60,960]{2,1,0:T(8,128)(2,1)S(1)} collective-permute-done((bf16[1,60,960]{2,1,0:T(8,128)(2,1)S(1)}, bf16[1,60,960]{2,1,0:T(8,128)(2,1)S(1)}, u32[]{:S(2)}, u32[]{:S(2)}) %collective-permute-start.39) | collective-permute-done | bytes 115232 | tf_op jit(solution)/shard_map/ppermute | solution.py:55
  474.7 3.2 collective-permute-start.40
  477.8 6.5 %collective-permute-done.59 = bf16[1,160,960]{2,1,0:T(8,128)(2,1)S(1)} collective-permute-done((bf16[1,160,960]{2,1,0:T(8,128)(2,1)S(1)}, bf16[1,160,960]{2,1,0:T(8,128)(2,1)S(1)}, u32[]{:S(2)}, u32[]{:S(2)}) %collective-permute-start.59) | collective-permute-done | bytes 307232 | tf_op jit(solution)/shard_map/ppermute | solution.py:55
  489.9 8.8 %collective-permute-done.60 = bf16[1,80,960]{2,1,0:T(8,128)(2,1)S(1)} collective-permute-done((bf16[1,80,960]{2,1,0:T(8,128)(2,1)S(1)}, bf16[1,80,960]{2,1,0:T(8,128)(2,1)S(1)}, u32[]{:S(2)}, u32[]{:S(2)}) %collective-permute-start.60) | collective-permute-done | bytes 153632 | tf_op jit(solution)/shard_map/ppermute | solution.py:55
  498.9 2.5 collective-permute-start.43
  503.2 6.0 collective-permute-done.61
  514.1 6.3 collective-permute-done.53
  520.6 7.5 %collective-permute-done.62 = bf16[1,160,960]{2,1,0:T(8,128)(2,1)S(1)} collective-permute-done((bf16[1,160,960]{2,1,0:T(8,128)(2,1)S(1)}, bf16[1,160,960]{2,1,0:T(8,128)(2,1)S(1)}, u32[]{:S(2)}, u32[]{:S(2)}) %collective-permute-start.62) | collective-permute-done | bytes 307232 | tf_op jit(solution)/shard_map/ppermute | solution.py:55
  530.2 3.1 collective-permute-done.54
  533.4 9.8 %collective-permute-done.48 = bf16[1,120,640]{2,1,0:T(8,128)(2,1)S(1)} collective-permute-done((bf16[1,120,640]{2,1,0:T(8,128)(2,1)S(1)}, bf16[1,120,640]{2,1,0:T(8,128)(2,1)S(1)}, u32[]{:S(2)}, u32[]{:S(2)}) %collective-permute-start.48) | collective-permute-done | bytes 153632 | tf_op jit(solution)/shard_map/ppermute | solution.py:55
  547.1 3.5 collective-permute-done.49
  558.8 2.4 copy.301
  561.2 4.4 collective-permute-start.64
  572.4 5.1 collective-permute-start.51
  582.1 4.6 collective-permute-start.58
  586.7 2.7 copy.302
  591.7 5.6 collective-permute-done.33
  597.4 3.0 fusion.5
  600.4 5.9 copy.308
  609.5 3.2 collective-permute-done.35
  615.7 6.6 %collective-permute-done.36 = bf16[1,120,1664]{2,1,0:T(8,128)(2,1)S(1)} collective-permute-done((bf16[1,120,1664]{2,1,0:T(8,128)(2,1)S(1)}, bf16[1,120,1664]{2,1,0:T(8,128)(2,1)S(1)}, u32[]{:S(2)}, u32[]{:S(2)}) %collective-permute-start.36) | collective-permute-done | bytes 399392 | tf_op jit(solution)/shard_map/ppermute | solution.py:55
  624.9 2.9 fusion.6
  627.8 2.9 fusion.7
  (561 shorter events, 222.9 us)
Async XLA Ops:
  7.2 128.4 %all-gather.2.cloned.1.call-start = ((), (), s32[]{:S(2)}) async-start(), calls=%async_computation | async-start | bytes 5570560 | tf_op jit(solution)/shard_map/all_gather | solution.py:340
  12.3 11.1 %collective-permute-start.1 = (bf16[120,1600]{1,0:T(8,128)(2,1)S(1)}, bf16[120,1600]{1,0:T(8,128)(2,1)S(1)}, u32[]{:S(2)}, u32[]{:S(2)}) collective-permute-start(bf16[120,1600]{1,0:T(8,128)(2,1)S(1)} %constant_dynamic-slice_fusion.9), channel_id=1, source_target_pairs={{0,1},{1,0},{2,3},{3,2},{4,5},{5,4},{6,7},{7,6},{8,9},{9,8},{10,11... | collective-permute-start | bytes 1152008 | tf_op jit(solution)/shard_map/ppermute | solution.py:59
  14.4 28.3 %collective-permute-start = (bf16[2,480]{1,0:T(2,128)(2,1)S(1)}, bf16[2,480]{1,0:T(2,128)(2,1)S(1)}, u32[]{:S(2)}, u32[]{:S(2)}) collective-permute-start(bf16[2,480]{1,0:T(2,128)(2,1)S(1)} %pad_maximum_fusion.51), channel_id=1, source_target_pairs={{0,1},{1,0},{2,3},{3,2},{4,5},{5,4},{6,7},{7,6},{8,9},{9,8},{10,11... | collective-permute-start | bytes 5768 | tf_op jit(solution)/shard_map/ppermute | solution.py:59
  23.4 9.6 %collective-permute-start.2 = (bf16[120,1600]{1,0:T(8,128)(2,1)S(1)}, bf16[120,1600]{1,0:T(8,128)(2,1)}, u32[]{:S(2)}, u32[]{:S(2)}) collective-permute-start(bf16[120,1600]{1,0:T(8,128)(2,1)S(1)} %collective-permute-done.1), channel_id=1, source_target_pairs={{0,4},{2,6},{4,0},{6,2},{8,12},{10,14},{12,8},{14,10},{16,20},{18,... | collective-permute-start | bytes 1152008 | tf_op jit(solution)/shard_map/ppermute | solution.py:55
  35.2 7.7 %collective-permute-start.3 = (bf16[240,1600]{1,0:T(8,128)(2,1)}, bf16[240,1600]{1,0:T(8,128)(2,1)}, u32[]{:S(2)}, u32[]{:S(2)}) collective-permute-start(bf16[240,1600]{1,0:T(8,128)(2,1)} %pad_maximum_fusion.36), channel_id=1, source_target_pairs={{0,2},{2,0},{4,6},{6,4},{8,10},{10,8},{12,14},{14,12},{16,18},{18,... | collective-permute-start | bytes 2304008 | tf_op jit(solution)/shard_map/ppermute | solution.py:55
  59.3 76.2 %collective-permute-start.4 = (bf16[120,2560]{1,0:T(8,128)(2,1)}, bf16[120,2560]{1,0:T(8,128)(2,1)}, u32[]{:S(2)}, u32[]{:S(2)}) collective-permute-start(bf16[120,2560]{1,0:T(8,128)(2,1)} %constant_dynamic-slice_fusion.8), channel_id=1, source_target_pairs={{0,1},{1,0},{2,3},{3,2},{4,5},{5,4},{6,7},{7,6},{8,9},{9,8},{10,11... | collective-permute-start | bytes 1843208 | tf_op jit(solution)/shard_map/ppermute | solution.py:59
  62.4 73.1 %collective-permute-start.5 = (bf16[120,2560]{1,0:T(8,128)(2,1)}, bf16[120,2560]{1,0:T(8,128)(2,1)}, u32[]{:S(2)}, u32[]{:S(2)}) collective-permute-start(bf16[120,2560]{1,0:T(8,128)(2,1)} %constant_dynamic-slice_fusion.7), channel_id=1, source_target_pairs={{0,1},{1,0},{2,3},{3,2},{4,5},{5,4},{6,7},{7,6},{8,9},{9,8},{10,11... | collective-permute-start | bytes 1843208 | tf_op jit(solution)/shard_map/ppermute | solution.py:59
  66.9 68.7 %collective-permute-start.6 = (bf16[320,960]{1,0:T(8,128)(2,1)}, bf16[320,960]{1,0:T(8,128)(2,1)}, u32[]{:S(2)}, u32[]{:S(2)}) collective-permute-start(bf16[320,960]{1,0:T(8,128)(2,1)} %constant_dynamic-slice_fusion.6), channel_id=1, source_target_pairs={{0,1},{1,0},{2,3},{3,2},{4,5},{5,4},{6,7},{7,6},{8,9},{9,8},{10,11... | collective-permute-start | bytes 1843208 | tf_op jit(solution)/shard_map/ppermute | solution.py:59
  69.0 38.6 %collective-permute-start.7 = (bf16[120,960]{1,0:T(8,128)(2,1)S(1)}, bf16[120,960]{1,0:T(8,128)(2,1)}, u32[]{:S(2)}, u32[]{:S(2)}) collective-permute-start(bf16[120,960]{1,0:T(8,128)(2,1)S(1)} %constant_dynamic-slice_fusion.5), channel_id=1, source_target_pairs={{0,1},{1,0},{2,3},{3,2},{4,5},{5,4},{6,7},{7,6},{8,9},{9,8},{10,11... | collective-permute-start | bytes 691208 | tf_op jit(solution)/shard_map/ppermute | solution.py:59
  107.6 7.0 %collective-permute-start.8 = (bf16[120,960]{1,0:T(8,128)(2,1)}, bf16[120,960]{1,0:T(8,128)(2,1)}, u32[]{:S(2)}, u32[]{:S(2)}) collective-permute-start(bf16[120,960]{1,0:T(8,128)(2,1)} %collective-permute-done.7), channel_id=1, source_target_pairs={{0,4},{2,6},{4,0},{6,2},{8,12},{10,14},{12,8},{14,10},{16,20},{18,... | collective-permute-start | bytes 691208 | tf_op jit(solution)/shard_map/ppermute | solution.py:55
  159.0 16.6 %collective-permute-start.14 = (bf16[320,960]{1,0:T(8,128)(2,1)}, bf16[320,960]{1,0:T(8,128)(2,1)S(1)}, u32[]{:S(2)}, u32[]{:S(2)}) collective-permute-start(bf16[320,960]{1,0:T(8,128)(2,1)} %collective-permute-done.6), channel_id=1, source_target_pairs={{0,4},{2,6},{4,0},{6,2},{8,12},{10,14},{12,8},{14,10},{16,20},{18,... | collective-permute-start | bytes 1843208 | tf_op jit(solution)/shard_map/ppermute | solution.py:55
  161.2 27.6 %collective-permute-start.12 = (bf16[120,2560]{1,0:T(8,128)(2,1)}, bf16[120,2560]{1,0:T(8,128)(2,1)}, u32[]{:S(2)}, u32[]{:S(2)}) collective-permute-start(bf16[120,2560]{1,0:T(8,128)(2,1)} %collective-permute-done.5), channel_id=1, source_target_pairs={{0,4},{2,6},{4,0},{6,2},{8,12},{10,14},{12,8},{14,10},{16,20},{18,... | collective-permute-start | bytes 1843208 | tf_op jit(solution)/shard_map/ppermute | solution.py:55
  161.6 40.4 %collective-permute-start.10 = (bf16[120,2560]{1,0:T(8,128)(2,1)}, bf16[120,2560]{1,0:T(8,128)(2,1)}, u32[]{:S(2)}, u32[]{:S(2)}) collective-permute-start(bf16[120,2560]{1,0:T(8,128)(2,1)} %collective-permute-done.4), channel_id=1, source_target_pairs={{0,4},{2,6},{4,0},{6,2},{8,12},{10,14},{12,8},{14,10},{16,20},{18,... | collective-permute-start | bytes 1843208 | tf_op jit(solution)/shard_map/ppermute | solution.py:55
  178.4 27.2 %collective-permute-start.15 = (bf16[640,960]{0,1:T(8,128)(2,1)}, bf16[640,960]{0,1:T(8,128)(2,1)}, u32[]{:S(2)}, u32[]{:S(2)}) collective-permute-start(bf16[640,960]{0,1:T(8,128)(2,1)} %copy.281), channel_id=1, source_target_pairs={{0,2},{2,0},{4,6},{6,4},{8,10},{10,8},{12,14},{14,12},{16,18},{18,... | collective-permute-start | bytes 3686408 | tf_op jit(solution)/shard_map/ppermute | solution.py:55
  191.4 23.5 %collective-permute-start.13 = (bf16[240,2560]{1,0:T(8,128)(2,1)}, bf16[240,2560]{1,0:T(8,128)(2,1)}, u32[]{:S(2)}, u32[]{:S(2)}) collective-permute-start(bf16[240,2560]{1,0:T(8,128)(2,1)} %pad_maximum_fusion.29), channel_id=1, source_target_pairs={{0,2},{2,0},{4,6},{6,4},{8,10},{10,8},{12,14},{14,12},{16,18},{18,... | collective-permute-start | bytes 3686408 | tf_op jit(solution)/shard_map/ppermute | solution.py:55
  204.7 12.1 %collective-permute-start.11 = (bf16[240,2560]{1,0:T(8,128)(2,1)}, bf16[240,2560]{1,0:T(8,128)(2,1)}, u32[]{:S(2)}, u32[]{:S(2)}) collective-permute-start(bf16[240,2560]{1,0:T(8,128)(2,1)} %pad_maximum_fusion.28), channel_id=1, source_target_pairs={{0,2},{2,0},{4,6},{6,4},{8,10},{10,8},{12,14},{14,12},{16,18},{18,... | collective-permute-start | bytes 3686408 | tf_op jit(solution)/shard_map/ppermute | solution.py:55
  246.2 22.3 %collective-permute-start.16 = (bf16[2,640,960]{1,2,0:T(8,128)(2,1)}, bf16[2,640,960]{1,2,0:T(8,128)(2,1)}, u32[]{:S(2)}, u32[]{:S(2)}) collective-permute-start(bf16[2,640,960]{1,2,0:T(8,128)(2,1)} %copy.290), channel_id=1, source_target_pairs={{0,2},{2,0},{4,6},{6,4},{8,10},{10,8},{12,14},{14,12},{16,18},{18,... | collective-permute-start | bytes 7372808 | tf_op jit(solution)/shard_map/ppermute | solution.py:55
  253.2 23.8 %collective-permute-start.17 = (bf16[2,480,1280]{2,1,0:T(8,128)(2,1)}, bf16[2,480,1280]{2,1,0:T(8,128)(2,1)}, u32[]{:S(2)}, u32[]{:S(2)}) collective-permute-start(bf16[2,480,1280]{2,1,0:T(8,128)(2,1)} %constant_dynamic-slice_fusion.3), channel_id=1, source_target_pairs={{0,2},{2,0},{4,6},{6,4},{8,10},{10,8},{12,14},{14,12},{16,18},{18,... | collective-permute-start | bytes 7372808 | tf_op jit(solution)/shard_map/ppermute | solution.py:55
  265.8 96.6 %collective-permute-start.25 = (bf16[2,480,1280]{2,1,0:T(8,128)(2,1)}, bf16[2,480,1280]{2,1,0:T(8,128)(2,1)}, u32[]{:S(2)}, u32[]{:S(2)}) collective-permute-start(bf16[2,480,1280]{2,1,0:T(8,128)(2,1)} %constant_dynamic-slice_fusion.2), channel_id=1, source_target_pairs={{0,2},{2,0},{4,6},{6,4},{8,10},{10,8},{12,14},{14,12},{16,18},{18,... | collective-permute-start | bytes 7372808 | tf_op jit(solution)/shard_map/ppermute | solution.py:55
  268.0 72.9 %collective-permute-start.27 = (bf16[2,240,960]{2,1,0:T(8,128)(2,1)}, bf16[2,240,960]{2,1,0:T(8,128)(2,1)}, u32[]{:S(2)}, u32[]{:S(2)}) collective-permute-start(bf16[2,240,960]{2,1,0:T(8,128)(2,1)} %constant_dynamic-slice_fusion.1), channel_id=1, source_target_pairs={{0,2},{2,0},{4,6},{6,4},{8,10},{10,8},{12,14},{14,12},{16,18},{18,... | collective-permute-start | bytes 2764808 | tf_op jit(solution)/shard_map/ppermute | solution.py:55
  285.1 28.8 %collective-permute-start.18 = (bf16[1,640,960]{1,2,0:T(8,128)(2,1)}, bf16[1,640,960]{1,2,0:T(8,128)(2,1)}, u32[]{:S(2)}, u32[]{:S(2)}) collective-permute-start(bf16[1,640,960]{1,2,0:T(8,128)(2,1)} %copy.293), channel_id=1, source_target_pairs={{0,1},{1,0},{2,3},{3,2},{4,5},{5,4},{6,7},{7,6},{8,9},{9,8},{10,11... | collective-permute-start | bytes 3686408 | tf_op jit(solution)/shard_map/ppermute | solution.py:59
  339.9 25.5 %collective-permute-start.19 = (bf16[2,8,128,640]{3,2,1,0:T(8,128)(2,1)}, bf16[2,8,128,640]{3,2,1,0:T(8,128)(2,1)}, u32[]{:S(2)}, u32[]{:S(2)}) collective-permute-start(bf16[2,8,128,640]{3,2,1,0:T(8,128)(2,1)} %dynamic-slice_bitcast_fusion), channel_id=1, source_target_pairs={{0,2},{2,0},{4,6},{6,4},{8,10},{10,8},{12,14},{14,12},{16,18},{18,... | collective-permute-start | bytes 7864328 | tf_op jit(solution)/shard_map/ppermute | solution.py:55
  344.0 13.0 %collective-permute-start.28 = (bf16[1,240,960]{2,1,0:T(8,128)(2,1)S(1)}, bf16[1,240,960]{2,1,0:T(8,128)(2,1)}, u32[]{:S(2)}, u32[]{:S(2)}) collective-permute-start(bf16[1,240,960]{2,1,0:T(8,128)(2,1)S(1)} %dynamic-slice_convert_fusion.9), channel_id=1, source_target_pairs={{0,1},{1,0},{2,3},{3,2},{4,5},{5,4},{6,7},{7,6},{8,9},{9,8},{10,11... | collective-permute-start | bytes 1382408 | tf_op jit(solution)/shard_map/ppermute | solution.py:59
  361.1 27.8 %collective-permute-start.24 = (bf16[1,480,1280]{2,1,0:T(8,128)(2,1)S(1)}, bf16[1,480,1280]{2,1,0:T(8,128)(2,1)S(1)}, u32[]{:S(2)}, u32[]{:S(2)}) collective-permute-start(bf16[1,480,1280]{2,1,0:T(8,128)(2,1)S(1)} %dynamic-slice_convert_fusion.3), channel_id=1, source_target_pairs={{0,1},{1,0},{2,3},{3,2},{4,5},{5,4},{6,7},{7,6},{8,9},{9,8},{10,11... | collective-permute-start | bytes 3686408 | tf_op jit(solution)/shard_map/ppermute | solution.py:59
  368.1 29.3 %collective-permute-start.20 = (bf16[2,4,128,640]{3,2,1,0:T(8,128)(2,1)S(1)}, bf16[2,4,128,640]{3,2,1,0:T(8,128)(2,1)S(1)}, u32[]{:S(2)}, u32[]{:S(2)}) collective-permute-start(bf16[2,4,128,640]{3,2,1,0:T(8,128)(2,1)S(1)} %fusion.13), channel_id=1, source_target_pairs={{0,4},{2,6},{4,0},{6,2},{8,12},{10,14},{12,8},{14,10},{16,20},{18,... | collective-permute-start | bytes 3932168 | tf_op jit(solution)/shard_map/ppermute | solution.py:55
  369.5 45.8 %collective-permute-start.26 = (bf16[1,480,1280]{2,1,0:T(8,128)(2,1)S(1)}, bf16[1,480,1280]{2,1,0:T(8,128)(2,1)S(1)}, u32[]{:S(2)}, u32[]{:S(2)}) collective-permute-start(bf16[1,480,1280]{2,1,0:T(8,128)(2,1)S(1)} %dynamic-slice_convert_fusion.2), channel_id=1, source_target_pairs={{0,1},{1,0},{2,3},{3,2},{4,5},{5,4},{6,7},{7,6},{8,9},{9,8},{10,11... | collective-permute-start | bytes 3686408 | tf_op jit(solution)/shard_map/ppermute | solution.py:59
  370.0 50.3 %collective-permute-start.23 = (bf16[1,320,960]{2,1,0:T(8,128)(2,1)S(1)}, bf16[1,320,960]{2,1,0:T(8,128)(2,1)S(1)}, u32[]{:S(2)}, u32[]{:S(2)}) collective-permute-start(bf16[1,320,960]{2,1,0:T(8,128)(2,1)S(1)} %dynamic-slice_convert_fusion.5), channel_id=1, source_target_pairs={{0,4},{2,6},{4,0},{6,2},{8,12},{10,14},{12,8},{14,10},{16,20},{18,... | collective-permute-start | bytes 1843208 | tf_op jit(solution)/shard_map/ppermute | solution.py:55
  397.7 19.3 %collective-permute-start.21 = (bf16[2,2,128,640]{3,2,1,0:T(8,128)(2,1)S(1)}, bf16[2,2,128,640]{3,2,1,0:T(8,128)(2,1)S(1)}, u32[]{:S(2)}, u32[]{:S(2)}) collective-permute-start(bf16[2,2,128,640]{3,2,1,0:T(8,128)(2,1)S(1)} %fusion.26), channel_id=1, source_target_pairs={{0,8},{2,10},{4,12},{6,14},{8,0},{10,2},{12,4},{14,6},{16,24},{18,... | collective-permute-start | bytes 1966088 | tf_op jit(solution)/shard_map/ppermute | solution.py:55
  417.2 16.6 %collective-permute-start.22 = (bf16[2,1,128,640]{3,2,1,0:T(8,128)(2,1)S(1)}, bf16[2,1,128,640]{3,2,1,0:T(8,128)(2,1)S(1)}, u32[]{:S(2)}, u32[]{:S(2)}) collective-permute-start(bf16[2,1,128,640]{3,2,1,0:T(8,128)(2,1)S(1)} %dynamic-slice_convert_fusion.12), channel_id=1, source_target_pairs={{0,16},{2,18},{4,20},{6,22},{8,24},{10,26},{12,28},{14,30},{16,0},... | collective-permute-start | bytes 983048 | tf_op jit(solution)/shard_map/ppermute | solution.py:55
  453.2 98.6 %collective-permute-start.29 = (bf16[2,240,1664]{2,1,0:T(8,128)(2,1)S(1)}, bf16[2,240,1664]{2,1,0:T(8,128)(2,1)S(1)}, u32[]{:S(2)}, u32[]{:S(2)}) collective-permute-start(bf16[2,240,1664]{2,1,0:T(8,128)(2,1)S(1)} %constant_dynamic-slice_fusion), channel_id=1, source_target_pairs={{0,2},{2,0},{4,6},{6,4},{8,10},{10,8},{12,14},{14,12},{16,18},{18,... | collective-permute-start | bytes 4792328 | tf_op jit(solution)/shard_map/ppermute | solution.py:55
  455.8 7.0 %collective-permute-start.38 = (bf16[1,120,960]{2,1,0:T(8,128)(2,1)S(1)}, bf16[1,120,960]{2,1,0:T(8,128)(2,1)S(1)}, u32[]{:S(2)}, u32[]{:S(2)}) collective-permute-start(bf16[1,120,960]{2,1,0:T(8,128)(2,1)S(1)} %dynamic-slice_convert_fusion.15), channel_id=1, source_target_pairs={{0,8},{2,10},{4,12},{6,14},{8,0},{10,2},{12,4},{14,6},{16,24},{18,... | collective-permute-start | bytes 691208 | tf_op jit(solution)/shard_map/ppermute | solution.py:55
  456.6 44.8 %collective-permute-start.45 = (bf16[1,480,640]{2,1,0:T(8,128)(2,1)S(1)}, bf16[1,480,640]{2,1,0:T(8,128)(2,1)S(1)}, u32[]{:S(2)}, u32[]{:S(2)}) collective-permute-start(bf16[1,480,640]{2,1,0:T(8,128)(2,1)S(1)} %dynamic-slice_convert_fusion.8), channel_id=1, source_target_pairs={{0,8},{2,10},{4,12},{6,14},{8,0},{10,2},{12,4},{14,6},{16,24},{18,... | collective-permute-start | bytes 1843208 | tf_op jit(solution)/shard_map/ppermute | solution.py:55
  457.5 45.4 %collective-permute-start.52 = (bf16[1,480,640]{2,1,0:T(8,128)(2,1)S(1)}, bf16[1,480,640]{2,1,0:T(8,128)(2,1)S(1)}, u32[]{:S(2)}, u32[]{:S(2)}) collective-permute-start(bf16[1,480,640]{2,1,0:T(8,128)(2,1)S(1)} %dynamic-slice_convert_fusion.7), channel_id=1, source_target_pairs={{0,4},{2,6},{4,0},{6,2},{8,12},{10,14},{12,8},{14,10},{16,20},{18,... | collective-permute-start | bytes 1843208 | tf_op jit(solution)/shard_map/ppermute | solution.py:55
  459.9 24.5 %collective-permute-start.59 = (bf16[1,160,960]{2,1,0:T(8,128)(2,1)S(1)}, bf16[1,160,960]{2,1,0:T(8,128)(2,1)S(1)}, u32[]{:S(2)}, u32[]{:S(2)}) collective-permute-start(bf16[1,160,960]{2,1,0:T(8,128)(2,1)S(1)} %dynamic-slice_convert_fusion.11), channel_id=1, source_target_pairs={{0,8},{2,10},{4,12},{6,14},{8,0},{10,2},{12,4},{14,6},{16,24},{18,... | collective-permute-start | bytes 921608 | tf_op jit(solution)/shard_map/ppermute | solution.py:55
  462.9 11.7 %collective-permute-start.39 = (bf16[1,60,960]{2,1,0:T(8,128)(2,1)S(1)}, bf16[1,60,960]{2,1,0:T(8,128)(2,1)S(1)}, u32[]{:S(2)}, u32[]{:S(2)}) collective-permute-start(bf16[1,60,960]{2,1,0:T(8,128)(2,1)S(1)} %dynamic-slice_convert_fusion.20), channel_id=1, source_target_pairs={{0,4},{2,6},{4,0},{6,2},{8,12},{10,14},{12,8},{14,10},{16,20},{18,... | collective-permute-start | bytes 345608 | tf_op jit(solution)/shard_map/ppermute | solution.py:55
  474.7 9.8 %collective-permute-start.40 = (bf16[1,30,960]{2,1,0:T(8,128)(2,1)S(1)}, bf16[1,30,960]{2,1,0:T(8,128)(2,1)S(1)}, u32[]{:S(2)}, u32[]{:S(2)}) collective-permute-start(bf16[1,30,960]{2,1,0:T(8,128)(2,1)S(1)} %dynamic-slice_convert_fusion.22), channel_id=1, source_target_pairs={{0,16},{2,18},{4,20},{6,22},{8,24},{10,26},{12,28},{14,30},{16,0},... | collective-permute-start | bytes 172808 | tf_op jit(solution)/shard_map/ppermute | solution.py:55
  486.6 12.0 %collective-permute-start.60 = (bf16[1,80,960]{2,1,0:T(8,128)(2,1)S(1)}, bf16[1,80,960]{2,1,0:T(8,128)(2,1)S(1)}, u32[]{:S(2)}, u32[]{:S(2)}) collective-permute-start(bf16[1,80,960]{2,1,0:T(8,128)(2,1)S(1)} %dynamic-slice_convert_fusion.17), channel_id=1, source_target_pairs={{0,16},{2,18},{4,20},{6,22},{8,24},{10,26},{12,28},{14,30},{16,0},... | collective-permute-start | bytes 460808 | tf_op jit(solution)/shard_map/ppermute | solution.py:55
  488.7 10.1 %collective-permute-start.42 = (bf16[1,60,960]{2,1,0:T(8,128)(2,1)S(1)}, bf16[1,60,960]{2,1,0:T(8,128)(2,1)S(1)}, u32[]{:S(2)}, u32[]{:S(2)}) collective-permute-start(bf16[1,60,960]{2,1,0:T(8,128)(2,1)S(1)} %pad_maximum_fusion.50), channel_id=1, source_target_pairs={{0,4},{2,6},{4,0},{6,2},{8,12},{10,14},{12,8},{14,10},{16,20},{18,... | collective-permute-start | bytes 345608 | tf_op jit(solution)/shard_map/ppermute | solution.py:55
  498.7 10.5 %collective-permute-start.61 = (bf16[1,80,960]{2,1,0:T(8,128)(2,1)S(1)}, bf16[1,80,960]{2,1,0:T(8,128)(2,1)S(1)}, u32[]{:S(2)}, u32[]{:S(2)}) collective-permute-start(bf16[1,80,960]{2,1,0:T(8,128)(2,1)S(1)} %reduce-precision_convert_fusion), channel_id=1, source_target_pairs={{0,16},{2,18},{4,20},{6,22},{8,24},{10,26},{12,28},{14,30},{16,0},... | collective-permute-start | bytes 460808 | tf_op jit(solution)/shard_map/ppermute | solution.py:55
  498.9 11.7 %collective-permute-start.43 = (bf16[1,120,960]{2,1,0:T(8,128)(2,1)S(1)}, bf16[1,120,960]{2,1,0:T(8,128)(2,1)S(1)}, u32[]{:S(2)}, u32[]{:S(2)}) collective-permute-start(bf16[1,120,960]{2,1,0:T(8,128)(2,1)S(1)} %pad_maximum_fusion.48), channel_id=1, source_target_pairs={{0,8},{2,10},{4,12},{6,14},{8,0},{10,2},{12,4},{14,6},{16,24},{18,... | collective-permute-start | bytes 691208 | tf_op jit(solution)/shard_map/ppermute | solution.py:55
  501.6 11.3 %collective-permute-start.46 = (bf16[1,240,640]{2,1,0:T(8,128)(2,1)S(1)}, bf16[1,240,640]{2,1,0:T(8,128)(2,1)S(1)}, u32[]{:S(2)}, u32[]{:S(2)}) collective-permute-start(bf16[1,240,640]{2,1,0:T(8,128)(2,1)S(1)} %dynamic-slice_convert_fusion.14), channel_id=1, source_target_pairs={{0,4},{2,6},{4,0},{6,2},{8,12},{10,14},{12,8},{14,10},{16,20},{18,... | collective-permute-start | bytes 921608 | tf_op jit(solution)/shard_map/ppermute | solution.py:55
  503.1 17.3 %collective-permute-start.53 = (bf16[1,240,640]{2,1,0:T(8,128)(2,1)S(1)}, bf16[1,240,640]{2,1,0:T(8,128)(2,1)S(1)}, u32[]{:S(2)}, u32[]{:S(2)}) collective-permute-start(bf16[1,240,640]{2,1,0:T(8,128)(2,1)S(1)} %dynamic-slice_convert_fusion.13), channel_id=1, source_target_pairs={{0,8},{2,10},{4,12},{6,14},{8,0},{10,2},{12,4},{14,6},{16,24},{18,... | collective-permute-start | bytes 921608 | tf_op jit(solution)/shard_map/ppermute | solution.py:55
  509.2 18.8 %collective-permute-start.62 = (bf16[1,160,960]{2,1,0:T(8,128)(2,1)S(1)}, bf16[1,160,960]{2,1,0:T(8,128)(2,1)S(1)}, u32[]{:S(2)}, u32[]{:S(2)}) collective-permute-start(bf16[1,160,960]{2,1,0:T(8,128)(2,1)S(1)} %pad_maximum_fusion.45), channel_id=1, source_target_pairs={{0,8},{2,10},{4,12},{6,14},{8,0},{10,2},{12,4},{14,6},{16,24},{18,... | collective-permute-start | bytes 921608 | tf_op jit(solution)/shard_map/ppermute | solution.py:55
  510.7 34.6 %collective-permute-start.44 = (bf16[1,240,960]{2,1,0:T(8,128)(2,1)S(1)}, bf16[1,240,960]{2,1,0:T(8,128)(2,1)S(1)}, u32[]{:S(2)}, u32[]{:S(2)}) collective-permute-start(bf16[1,240,960]{2,1,0:T(8,128)(2,1)S(1)} %pad_maximum_fusion.42), channel_id=1, source_target_pairs={{0,2},{2,0},{4,6},{6,4},{8,10},{10,8},{12,14},{14,12},{16,18},{18,... | collective-permute-start | bytes 1382408 | tf_op jit(solution)/shard_map/ppermute | solution.py:55
  513.0 16.6 %collective-permute-start.47 = (bf16[1,120,640]{2,1,0:T(8,128)(2,1)S(1)}, bf16[1,120,640]{2,1,0:T(8,128)(2,1)S(1)}, u32[]{:S(2)}, u32[]{:S(2)}) collective-permute-start(bf16[1,120,640]{2,1,0:T(8,128)(2,1)S(1)} %dynamic-slice_convert_fusion.19), channel_id=1, source_target_pairs={{0,16},{2,18},{4,20},{6,22},{8,24},{10,26},{12,28},{14,30},{16,0},... | collective-permute-start | bytes 460808 | tf_op jit(solution)/shard_map/ppermute | solution.py:55
  520.5 12.8 %collective-permute-start.54 = (bf16[1,120,640]{2,1,0:T(8,128)(2,1)S(1)}, bf16[1,120,640]{2,1,0:T(8,128)(2,1)S(1)}, u32[]{:S(2)}, u32[]{:S(2)}) collective-permute-start(bf16[1,120,640]{2,1,0:T(8,128)(2,1)S(1)} %dynamic-slice_convert_fusion.18), channel_id=1, source_target_pairs={{0,16},{2,18},{4,20},{6,22},{8,24},{10,26},{12,28},{14,30},{16,0},... | collective-permute-start | bytes 460808 | tf_op jit(solution)/shard_map/ppermute | solution.py:55
  528.3 27.9 %collective-permute-start.63 = (bf16[1,320,960]{2,1,0:T(8,128)(2,1)S(1)}, bf16[1,320,960]{2,1,0:T(8,128)(2,1)S(1)}, u32[]{:S(2)}, u32[]{:S(2)}) collective-permute-start(bf16[1,320,960]{2,1,0:T(8,128)(2,1)S(1)} %pad_maximum_fusion.38), channel_id=1, source_target_pairs={{0,4},{2,6},{4,0},{6,2},{8,12},{10,14},{12,8},{14,10},{16,20},{18,... | collective-permute-start | bytes 1843208 | tf_op jit(solution)/shard_map/ppermute | solution.py:55
  529.6 13.6 %collective-permute-start.48 = (bf16[1,120,640]{2,1,0:T(8,128)(2,1)S(1)}, bf16[1,120,640]{2,1,0:T(8,128)(2,1)S(1)}, u32[]{:S(2)}, u32[]{:S(2)}) collective-permute-start(bf16[1,120,640]{2,1,0:T(8,128)(2,1)S(1)} %reduce-precision_convert_fusion.2), channel_id=1, source_target_pairs={{0,16},{2,18},{4,20},{6,22},{8,24},{10,26},{12,28},{14,30},{16,0},... | collective-permute-start | bytes 460808 | tf_op jit(solution)/shard_map/ppermute | solution.py:55
  533.3 11.9 %collective-permute-start.55 = (bf16[1,120,640]{2,1,0:T(8,128)(2,1)S(1)}, bf16[1,120,640]{2,1,0:T(8,128)(2,1)S(1)}, u32[]{:S(2)}, u32[]{:S(2)}) collective-permute-start(bf16[1,120,640]{2,1,0:T(8,128)(2,1)S(1)} %reduce-precision_convert_fusion.1), channel_id=1, source_target_pairs={{0,16},{2,18},{4,20},{6,22},{8,24},{10,26},{12,28},{14,30},{16,0},... | collective-permute-start | bytes 460808 | tf_op jit(solution)/shard_map/ppermute | solution.py:55
  543.3 7.2 %collective-permute-start.49 = (bf16[1,240,640]{2,1,0:T(8,128)(2,1)S(1)}, bf16[1,240,640]{2,1,0:T(8,128)(2,1)S(1)}, u32[]{:S(2)}, u32[]{:S(2)}) collective-permute-start(bf16[1,240,640]{2,1,0:T(8,128)(2,1)S(1)} %pad_maximum_fusion.46), channel_id=1, source_target_pairs={{0,4},{2,6},{4,0},{6,2},{8,12},{10,14},{12,8},{14,10},{16,20},{18,... | collective-permute-start | bytes 921608 | tf_op jit(solution)/shard_map/ppermute | solution.py:55
  545.3 6.4 collective-permute-start.56
  551.6 14.0 %collective-permute-start.50 = (bf16[1,480,640]{2,1,0:T(8,128)(2,1)}, bf16[1,480,640]{2,1,0:T(8,128)(2,1)}, u32[]{:S(2)}, u32[]{:S(2)}) collective-permute-start(bf16[1,480,640]{2,1,0:T(8,128)(2,1)} %pad_maximum_fusion.39), channel_id=1, source_target_pairs={{0,8},{2,10},{4,12},{6,14},{8,0},{10,2},{12,4},{14,6},{16,24},{18,... | collective-permute-start | bytes 1843208 | tf_op jit(solution)/shard_map/ppermute | solution.py:55
  553.1 16.2 %collective-permute-start.30 = (bf16[1,240,1664]{2,1,0:T(8,128)(2,1)}, bf16[1,240,1664]{2,1,0:T(8,128)(2,1)}, u32[]{:S(2)}, u32[]{:S(2)}) collective-permute-start(bf16[1,240,1664]{2,1,0:T(8,128)(2,1)} %dynamic-slice_convert_fusion.4), channel_id=1, source_target_pairs={{0,1},{1,0},{2,3},{3,2},{4,5},{5,4},{6,7},{7,6},{8,9},{9,8},{10,11... | collective-permute-start | bytes 2396168 | tf_op jit(solution)/shard_map/ppermute | solution.py:59
  555.3 22.2 %collective-permute-start.57 = (bf16[1,480,640]{2,1,0:T(8,128)(2,1)}, bf16[1,480,640]{2,1,0:T(8,128)(2,1)}, u32[]{:S(2)}, u32[]{:S(2)}) collective-permute-start(bf16[1,480,640]{2,1,0:T(8,128)(2,1)} %pad_maximum_fusion.40), channel_id=1, source_target_pairs={{0,4},{2,6},{4,0},{6,2},{8,12},{10,14},{12,8},{14,10},{16,20},{18,... | collective-permute-start | bytes 1843208 | tf_op jit(solution)/shard_map/ppermute | solution.py:55
  561.2 25.5 %collective-permute-start.64 = (bf16[1,640,960]{1,2,0:T(8,128)(2,1)}, bf16[1,640,960]{1,2,0:T(8,128)(2,1)}, u32[]{:S(2)}, u32[]{:S(2)}) collective-permute-start(bf16[1,640,960]{1,2,0:T(8,128)(2,1)} %copy.301), channel_id=1, source_target_pairs={{0,2},{2,0},{4,6},{6,4},{8,10},{10,8},{12,14},{14,12},{16,18},{18,... | collective-permute-start | bytes 3686408 | tf_op jit(solution)/shard_map/ppermute | solution.py:55
  570.7 8.1 %collective-permute-start.31 = (bf16[1,120,1664]{2,1,0:T(8,128)(2,1)S(1)}, bf16[1,120,1664]{2,1,0:T(8,128)(2,1)S(1)}, u32[]{:S(2)}, u32[]{:S(2)}) collective-permute-start(bf16[1,120,1664]{2,1,0:T(8,128)(2,1)S(1)} %dynamic-slice_convert_fusion.10), channel_id=1, source_target_pairs={{0,4},{2,6},{4,0},{6,2},{8,12},{10,14},{12,8},{14,10},{16,20},{18,... | collective-permute-start | bytes 1198088 | tf_op jit(solution)/shard_map/ppermute | solution.py:55
  572.4 35.4 %collective-permute-start.51 = (bf16[1,480,1280]{2,1,0:T(8,128)(2,1)}, bf16[1,480,1280]{2,1,0:T(8,128)(2,1)}, u32[]{:S(2)}, u32[]{:S(2)}) collective-permute-start(bf16[1,480,1280]{2,1,0:T(8,128)(2,1)} %pad_maximum_fusion.30), channel_id=1, source_target_pairs={{0,2},{2,0},{4,6},{6,4},{8,10},{10,8},{12,14},{14,12},{16,18},{18,... | collective-permute-start | bytes 3686408 | tf_op jit(solution)/shard_map/ppermute | solution.py:55
  579.6 9.7 %collective-permute-start.32 = (bf16[1,60,1664]{2,1,0:T(8,128)(2,1)}, bf16[1,60,1664]{2,1,0:T(8,128)(2,1)S(1)}, u32[]{:S(2)}, u32[]{:S(2)}) collective-permute-start(bf16[1,60,1664]{2,1,0:T(8,128)(2,1)} %dynamic-slice_convert_fusion.16), channel_id=1, source_target_pairs={{0,8},{2,10},{4,12},{6,14},{8,0},{10,2},{12,4},{14,6},{16,24},{18,... | collective-permute-start | bytes 599048 | tf_op jit(solution)/shard_map/ppermute | solution.py:55
  582.1 31.8 %collective-permute-start.58 = (bf16[1,480,1280]{2,1,0:T(8,128)(2,1)}, bf16[1,480,1280]{2,1,0:T(8,128)(2,1)}, u32[]{:S(2)}, u32[]{:S(2)}) collective-permute-start(bf16[1,480,1280]{2,1,0:T(8,128)(2,1)} %pad_maximum_fusion.31), channel_id=1, source_target_pairs={{0,2},{2,0},{4,6},{6,4},{8,10},{10,8},{12,14},{14,12},{16,18},{18,... | collective-permute-start | bytes 3686408 | tf_op jit(solution)/shard_map/ppermute | solution.py:55
  589.5 7.8 %collective-permute-start.33 = (bf16[1,30,1664]{2,1,0:T(8,128)(2,1)S(1)}, bf16[1,30,1664]{2,1,0:T(8,128)(2,1)S(1)}, u32[]{:S(2)}, u32[]{:S(2)}) collective-permute-start(bf16[1,30,1664]{2,1,0:T(8,128)(2,1)S(1)} %dynamic-slice_convert_fusion.21), channel_id=1, source_target_pairs={{0,16},{2,18},{4,20},{6,22},{8,24},{10,26},{12,28},{14,30},{16,0},... | collective-permute-start | bytes 299528 | tf_op jit(solution)/shard_map/ppermute | solution.py:55
  597.3 8.9 %collective-permute-start.34 = (bf16[1,30,1664]{2,1,0:T(8,128)(2,1)S(1)}, bf16[1,30,1664]{2,1,0:T(8,128)(2,1)S(1)}, u32[]{:S(2)}, u32[]{:S(2)}) collective-permute-start(bf16[1,30,1664]{2,1,0:T(8,128)(2,1)S(1)} %reduce-precision_convert_fusion.3), channel_id=1, source_target_pairs={{0,16},{2,18},{4,20},{6,22},{8,24},{10,26},{12,28},{14,30},{16,0},... | collective-permute-start | bytes 299528 | tf_op jit(solution)/shard_map/ppermute | solution.py:55
  606.3 6.4 collective-permute-start.35
  612.9 9.4 %collective-permute-start.36 = (bf16[1,120,1664]{2,1,0:T(8,128)(2,1)S(1)}, bf16[1,120,1664]{2,1,0:T(8,128)(2,1)S(1)}, u32[]{:S(2)}, u32[]{:S(2)}) collective-permute-start(bf16[1,120,1664]{2,1,0:T(8,128)(2,1)S(1)} %pad_maximum_fusion.43), channel_id=1, source_target_pairs={{0,4},{2,6},{4,0},{6,2},{8,12},{10,14},{12,8},{14,10},{16,20},{18,... | collective-permute-start | bytes 1198088 | tf_op jit(solution)/shard_map/ppermute | solution.py:55
  622.6 8.1 %collective-permute-start.37 = (bf16[1,240,1664]{2,1,0:T(8,128)(2,1)S(1)}, bf16[1,240,1664]{2,1,0:T(8,128)(2,1)S(1)}, u32[]{:S(2)}, u32[]{:S(2)}) collective-permute-start(bf16[1,240,1664]{2,1,0:T(8,128)(2,1)S(1)} %pad_maximum_fusion.37), channel_id=1, source_target_pairs={{0,2},{2,0},{4,6},{6,4},{8,10},{10,8},{12,14},{14,12},{16,18},{18,... | collective-permute-start | bytes 2396168 | tf_op jit(solution)/shard_map/ppermute | solution.py:55
  (119 other events, 954.3 us)
Sparse Core Ops, SparseCore 0:
  57.5 57.1 all-gather.1
